TPU v7x, 128 devices: a whole 4x4x4 slice. The times are simulated.
128 devices in a mesh: lon: 16 (over y, z), lat: 8 (over x, core).
Axes of the slice: x: 4, y: 4, z: 4, core: 2. Of those that a mesh axis runs over, the one named last changes fastest.
Arguments:
- layers: float32 [6, 100, 256, 2048], P(None, None, 'lat', 'lon'), may hold values from -4 to 4, as said below
- kmt: int32 [256, 2048], P('lat', 'lon'), may hold values from 0 to 100, as said below
- barotropic: float32 [3, 256, 2048], P(None, 'lat', 'lon'), may hold values from -3 to 3
Outputs:
- layers_new: float32 [6, 100, 256, 2048], P(None, None, 'lat', 'lon')
- barotropic_new: float32 [3, 256, 2048], P(None, 'lat', 'lon')
Inputs may be any that keep to these rules, and one draw needn't show every extreme that they name: kmt is 0 on the first and the last row of the grid, on whole land blocks of 8 x 16 columns and on scattered coastal columns; elsewhere it is 1 to 100. `layers`: component 2 (thickness) lies between 0.5 and 2.
All inputs are finite; a program needn't handle non-finite values.
Results may differ from a plain program's by a relative error of at most 0.00002.
Values sent between devices are 32-bit elements; how exact they have to be, the bound alone decides.
A program may use at most 256 MiB of HBM per device.

v0:
```python
import jax
import jax.numpy as jnp
from jax import lax
from jax.sharding import PartitionSpec as P

K = 100
NSUB = 16


time_step = 0.1
sub_step = 0.6
hyper_visc = 0.01
diffusivity = 0.1
gravity = 0.1
thermal = 1.0
haline = 0.8
rotation = 0.5


def extended(block, sides, width):
    for axis, dim in sides:
        count = lax.axis_size(axis)
        forward = [(i, i + 1) for i in range(count - 1)]
        forward.append((count - 1, 0))
        backward = [(target, source) for source, target in forward]
        low = lax.ppermute(
            lax.slice_in_dim(block, block.shape[dim] - width, None, axis=dim), axis, forward
        )
        high = lax.ppermute(lax.slice_in_dim(block, 0, width, axis=dim), axis, backward)
        block = jnp.concatenate([low, block, high], axis=dim)
    return block


def trim_rim(field, width):
    return field[..., width:-width, width:-width]


def east_diff(field):
    return 0.5 * (field[..., 1:-1, 2:] - field[..., 1:-1, :-2])


def north_diff(field):
    return 0.5 * (field[..., 2:, 1:-1] - field[..., :-2, 1:-1])


def laplace(field):
    return (
        field[..., 2:, 1:-1]
        + field[..., :-2, 1:-1]
        + field[..., 1:-1, 2:]
        + field[..., 1:-1, :-2]
        - 4.0 * field[..., 1:-1, 1:-1]
    )


def pressure(thick, temper, saline):
    weight = gravity * (haline * saline - thermal * temper) * thick
    return jnp.cumsum(weight, axis=0) - 0.5 * weight


def depth_mean(values, thick, column_total):
    return jnp.sum(values * thick, axis=-3) / jnp.maximum(column_total, 1.0)


def baroclinic(vel_wide, scalar_wide, level_mask, coriolis):
    press = pressure(scalar_wide[0], scalar_wide[1], scalar_wide[2])
    velocity = trim_rim(vel_wide, 2)
    thick = trim_rim(scalar_wide[0], 1)
    column_total = jnp.sum(thick, axis=0)
    tend_east = (
        -east_diff(press) + coriolis * velocity[1] - hyper_visc * laplace(laplace(vel_wide[0]))
    ) * level_mask
    tend_north = (
        -north_diff(press) - coriolis * velocity[0] - hyper_visc * laplace(laplace(vel_wide[1]))
    ) * level_mask
    tendency = jnp.stack([tend_east, tend_north])
    forcing = depth_mean(tendency, thick, column_total)
    provisional = (velocity + time_step * (tendency - forcing[:, None])) * level_mask
    clinic = (provisional - depth_mean(provisional, thick, column_total)[:, None]) * level_mask
    return (clinic, forcing, column_total / K)


def transport(thick, tracer, flow_wide, scalar_wide, level_mask):
    thick_wide = scalar_wide[0]
    tracer_wide = scalar_wide[1:4]
    flux_east = thick_wide * flow_wide[0]
    flux_north = thick_wide * flow_wide[1]
    thick_new = (thick - time_step * (east_diff(flux_east) + north_diff(flux_north))) * level_mask
    content = (
        thick * tracer
        - time_step * (east_diff(flux_east * tracer_wide) + north_diff(flux_north * tracer_wide))
        + time_step * diffusivity * laplace(tracer_wide)
    ) * level_mask
    return (thick_new, content)


def per_device(layers, kmt, barotropic):
    rows_local, cols_local = kmt.shape
    levels = jnp.arange(K, dtype=jnp.int32)[:, None, None]
    level_mask = (levels < kmt[None]).astype(jnp.float32)
    column_mask = (kmt > 0).astype(jnp.float32)
    fields = layers * level_mask
    total_rows = rows_local * lax.axis_size("lat")
    rows_global = (
        lax.axis_index("lat") * rows_local + jnp.arange(rows_local, dtype=jnp.int32)
    ).astype(jnp.float32)
    coriolis = (rotation * (2.0 * (rows_global + 0.5) / total_rows - 1.0))[:, None]
    widened = extended(fields, (("lat", 2), ("lon", 3)), 2)
    vel_wide = widened[0:2]
    scalar_wide = widened[2:6, :, 1:-1, 1:-1]
    clinic, forcing, depth_bar = baroclinic(vel_wide, scalar_wide, level_mask, coriolis)
    surface = barotropic * column_mask

    def subcycle(step, carry):
        height, east, north, sum_east, sum_north = carry
        flux_wide = extended(
            jnp.stack([depth_bar * east, depth_bar * north]), (("lat", 1), ("lon", 2)), 1
        )
        height = (
            height - sub_step * (east_diff(flux_wide[0]) + north_diff(flux_wide[1]))
        ) * column_mask
        height_wide = extended(height, (("lat", 0), ("lon", 1)), 1)
        east = (east + sub_step * (forcing[0] - east_diff(height_wide))) * column_mask
        north = (north + sub_step * (forcing[1] - north_diff(height_wide))) * column_mask
        return (height, east, north, sum_east + east, sum_north + north)

    zeros = jnp.zeros_like(surface[0])
    final = lax.fori_loop(0, NSUB, subcycle, (surface[0], surface[1], surface[2], zeros, zeros))
    state = jnp.stack([final[0], final[1], final[2]])
    sum_flow = jnp.stack([final[3], final[4]])
    mean_flow = sum_flow / NSUB
    vel_new = (clinic + mean_flow[:, None]) * level_mask
    flow_wide = extended(vel_new, (("lat", 2), ("lon", 3)), 1)
    thick_new, content = transport(fields[2], fields[3:6], flow_wide, scalar_wide, level_mask)
    layers_new = jnp.concatenate([vel_new, thick_new[None], content], axis=0)
    return (layers_new, state)


def solution(mesh):
    return jax.shard_map(
        per_device,
        mesh=mesh,
        in_specs=(P(None, None, "lat", "lon"), P("lat", "lon"), P(None, "lat", "lon")),
        out_specs=(P(None, None, "lat", "lon"), P(None, "lat", "lon")),
        check_vma=False,
    )
```

profile of v0, /device:TPU:0, one launch (start us, length us, event | category | flops | bytes accessed | tf_op | source)
XLA Modules:
  0.0 770.6 jit_solution(14656523027025932230)
XLA Ops:
  1.6 6.8 broadcast_multiply_fusion
  15.7 7.8 %collective-permute-done.8 = f32[6,100,2,128]{3,2,1,0:T(2,128)S(1)} collective-permute-done((f32[6,100,2,128]{3,2,1,0:T(2,128)S(1)}, f32[6,100,2,128]{3,2,1,0:T(2,128)S(1)}, u32[]{:S(2)}, u32[]{:S(2)}) %collective-permute-start.8) | collective-permute-done | bytes 614432 | tf_op jit(solution)/shard_map/ppermute | solution.py:26
  23.5 5.5 pad_maximum_fusion.14
  29.1 9.6 %fusion.63 = (f32[6,100,36,2]{3,2,1,0:T(8,128)}, f32[6,100,36,2]{3,2,1,0:T(8,128)}) fusion(f32[6,100,36,128]{3,2,1,0:T(8,128)S(1)} %pad_maximum_fusion.14), kind=kLoop, calls=%fused_computation.151 | loop fusion | bytes 691200 | tf_op jit(solution)/shard_map/slice | solution.py:29
  38.6 7.7 copy.5
  48.4 7.7 %copy.6 = f32[6,100,36,2]{1,3,2,0:T(2,128)S(1)} copy(f32[6,100,36,2]{3,2,1,0:T(8,128)} %get-tuple-element.198) | data formatting | bytes 345600 | tf_op jit(solution)/shard_map/slice | solution.py:29
  60.8 7.2 copy.7
  67.9 7.3 copy.8
  75.2 26.0 %pad_maximum_fusion.13 = f32[6,100,36,132]{3,2,1,0:T(8,128)} fusion(f32[6,100,36,2]{3,2,1,0:T(8,128)} %copy.8, f32[6,100,2,128]{3,2,1,0:T(2,128)S(1)} %collective-permute-done.9, f32[6,100,32,128]{3,2,1,0:T(8,128)} %copy-done, f32[6,100,2,128]{3,2,1,0:T(2,128)S(1)} %collective-permute-done.8, f32[6,100,36,2]{3,2,1,0:T(8,128)} %copy.7), kind=kLoop, calls=%fused_computation.37 | loop fusion | flops 11404800 | bytes 22809600 | tf_op jit(solution)/shard_map/concatenate | solution.py:30
  101.2 7.1 slice_bitcast_fusion.3
  108.3 37.0 %multiply_subtract_fusion = f32[100,34,130]{2,1,0:T(8,128)} fusion(f32[6,100,36,132]{3,2,1,0:T(8,128)} %pad_maximum_fusion.13), kind=kOutput, calls=%fused_computation.86 | output fusion | flops 48178000 | bytes 13172800 | tf_op jit(solution)/shard_map/jit(cumsum)/reduce_window_sum | solution.py:58
  151.2 10.6 %fusion.26 = (f32[100,34,130]{2,1,0:T(8,128)}, f32[100,34,130]{2,1,0:T(8,128)}) fusion(f32[100,36,132]{2,1,0:T(8,128)S(1)} %copy-done.2, f32[100,36,132]{2,1,0:T(8,128)S(1)} %copy-done.1), kind=kLoop, calls=%fused_computation.65 | loop fusion | flops 4420000 | bytes 21216000 | tf_op jit(solution)/shard_map/sub | solution.py:48
  161.8 22.5 %fusion.50 = (f32[1,100,32,128]{3,2,1,0:T(8,128)S(1)}, f32[1,100,32,128]{3,2,1,0:T(8,128)S(1)}) fusion(f32[100,34,130]{2,1,0:T(8,128)} %get-tuple-element.214, f32[6,100,32,128]{3,2,1,0:T(8,128)} %copy-done, f32[100,34,130]{2,1,0:T(8,128)} %multiply_subtract_fusion, f32[32]{0:T(128)S(1)} %add_multiply_fusion.1, s32[32,128]{1,0:T(8,128)} %param.6, ...), kind=kLoop, calls=%fused_computation.122 | loop fusion | flops 11059200 | bytes 29507712 | tf_op jit(solution)/shard_map/stack | solution.py:76
  191.7 461.0 %while.21 = (s32[]{:T(128)}, f32[32,128]{1,0:T(8,128)S(1)}, f32[32,128]{1,0:T(8,128)S(1)}, f32[32,128]{1,0:T(8,128)S(1)}, f32[32,128]{1,0:T(8,128)S(1)}, /*index...) while((s32[]{:T(128)}, f32[32,128]{1,0:T(8,128)S(1)}, ...), condition=%wide.region_5.6_spmd.clone, body=%wide.region_4.5_spmd.clone.sunk | while | flops 210603 | bytes 728680 | solution.py:128
  203.4 5.6 collective-permute-done.3
  225.2 5.4 collective-permute-start.2
  232.2 5.6 collective-permute-done.3
  253.9 5.4 collective-permute-start.2
  261.0 5.6 collective-permute-done.3
  282.7 5.4 collective-permute-start.2
  289.8 5.6 collective-permute-done.3
  311.5 5.4 collective-permute-start.2
  318.6 5.6 collective-permute-done.3
  340.3 5.4 collective-permute-start.2
  347.4 5.6 collective-permute-done.3
  369.1 5.4 collective-permute-start.2
  376.2 5.6 collective-permute-done.3
  397.9 5.4 collective-permute-start.2
  405.0 5.6 collective-permute-done.3
  433.8 5.6 collective-permute-done.3
  455.5 5.4 collective-permute-start.2
  462.5 5.6 collective-permute-done.3
  484.3 5.4 collective-permute-start.2
  491.3 5.6 collective-permute-done.3
  513.1 5.4 collective-permute-start.2
  520.1 5.6 collective-permute-done.3
  548.9 5.6 collective-permute-done.3
  577.7 5.6 collective-permute-done.3
  606.5 5.6 collective-permute-done.3
  628.3 5.4 collective-permute-start.2
  635.3 5.6 collective-permute-done.3
  690.1 9.8 %pad_maximum_fusion.16 = f32[2,100,34,130]{3,2,1,0:T(8,128)} fusion(f32[2,100,34,1]{3,2,1,0:T(8,128)} %copy.12, f32[2,100,1,128]{3,2,1,0:T(1,128)S(1)} %copy-done.14, f32[2,100,32,128]{3,2,1,0:T(8,128)S(1)} %add_multiply_fusion, f32[2,100,1,128]{3,2,1,0:T(1,128)S(1)} %collective-permute-done.12, f32[2,100,34,1]{3,2,1,0:T(8,128)} %copy.11), kind=kLoop, calls=%fused_computation.42 | loop fusion | flops 3536000 | bytes 7072000 | tf_op jit(solution)/shard_map/concatenate | solution.py:30
  699.8 9.1 %bitcast_multiply_fusion.1 = (f32[100,34,130]{2,1,0:T(8,128)}, f32[100,34,130]{2,1,0:T(8,128)}) fusion(f32[2,100,34,130]{3,2,1,0:T(8,128)} %pad_maximum_fusion.16, f32[6,100,36,132]{3,2,1,0:T(8,128)} %pad_maximum_fusion.13), kind=kLoop, calls=%fused_computation.83 | loop fusion | flops 884000 | bytes 8840000 | tf_op jit(solution)/shard_map/mul | solution.py:86
  709.0 7.8 %multiply_bitcast_fusion.3 = (f32[100,34,130]{2,1,0:T(8,128)S(1)}, f32[100,34,130]{2,1,0:T(8,128)}) fusion(f32[2,100,34,130]{3,2,1,0:T(8,128)} %pad_maximum_fusion.16, f32[6,100,36,132]{3,2,1,0:T(8,128)} %pad_maximum_fusion.13), kind=kLoop, calls=%fused_computation.85 | loop fusion | flops 884000 | bytes 8840000 | tf_op jit(solution)/shard_map/mul | solution.py:91
  716.8 7.7 fusion.36
  724.5 13.1 %slice_multiply_fusion.1 = (f32[3,100,34,130]{3,2,1,0:T(8,128)}, f32[3,100,34,130]{3,2,1,0:T(8,128)}) fusion(f32[6,100,36,132]{3,2,1,0:T(8,128)} %pad_maximum_fusion.13, f32[100,34,130]{2,1,0:T(8,128)S(1)} %get-tuple-element.190, f32[100,34,130]{2,1,0:T(8,128)S(1)} %copy-done.9), kind=kLoop, calls=%fused_computation.40 | loop fusion | flops 2652000 | bytes 19448000 | tf_op jit(solution)/shard_map/mul | solution.py:91
  737.6 22.5 %fusion.20 = f32[3,100,32,128]{3,2,1,0:T(8,128)} fusion(f32[6,100,36,2]{3,2,1,0:T(8,128)} %copy.7, f32[6,100,2,128]{3,2,1,0:T(2,128)} %copy-done.12, f32[6,100,32,128]{3,2,1,0:T(8,128)S(1)} %bitcast.90, f32[6,100,2,128]{3,2,1,0:T(2,128)} %copy-done.11, f32[6,100,36,2]{3,2,1,0:T(8,128)} %copy.8, f32[3,100,34,130]{3,2,1,0:T(8,128)} %get-tuple-element.193, ...), kind=kLoop, calls=%fused_computation.48 | loop fusion | flops 27033600 | bytes 44172800 | tf_op jit(solution)/shard_map/mul | solution.py:89
  760.1 10.0 %pad_maximum_fusion.15 = f32[6,100,32,128]{3,2,1,0:T(8,128)} fusion(f32[3,100,32,128]{3,2,1,0:T(8,128)} %fusion.20, f32[1,100,32,128]{3,2,1,0:T(8,128)} %fusion.36, f32[2,100,32,128]{3,2,1,0:T(8,128)} %copy-done.3), kind=kLoop, calls=%fused_computation.41 | loop fusion | flops 4915200 | bytes 19660800 | tf_op jit(solution)/shard_map/concatenate | solution.py:135
  (507 shorter events, 375.4 us)
Async XLA Ops:
  12.7 10.8 %collective-permute-start.8 = (f32[6,100,2,128]{3,2,1,0:T(2,128)S(1)}, f32[6,100,2,128]{3,2,1,0:T(2,128)S(1)}, u32[]{:S(2)}, u32[]{:S(2)}) collective-permute-start(f32[6,100,2,128]{3,2,1,0:T(2,128)S(1)} %get-tuple-element.200), channel_id=1, source_target_pairs={{0,1},{1,2},{2,3},{3,4},{4,5},{5,6},{6,7},{7,0},{8,9},{9,10},{10,1... | collective-permute-start | bytes 1843208 | tf_op jit(solution)/shard_map/ppermute | solution.py:26
  12.7 10.8 %collective-permute-start.9 = (f32[6,100,2,128]{3,2,1,0:T(2,128)S(1)}, f32[6,100,2,128]{3,2,1,0:T(2,128)S(1)}, u32[]{:S(2)}, u32[]{:S(2)}) collective-permute-start(f32[6,100,2,128]{3,2,1,0:T(2,128)S(1)} %get-tuple-element.201), channel_id=1, source_target_pairs={{1,0},{2,1},{3,2},{4,3},{5,4},{6,5},{7,6},{0,7},{9,8},{10,9},{11,1... | collective-permute-start | bytes 1843208 | tf_op jit(solution)/shard_map/ppermute | solution.py:29
  46.3 14.5 %collective-permute-start.10 = (f32[6,100,36,2]{1,3,2,0:T(2,128)S(1)}, f32[6,100,36,2]{1,3,2,0:T(2,128)S(1)}, u32[]{:S(2)}, u32[]{:S(2)}) collective-permute-start(f32[6,100,36,2]{1,3,2,0:T(2,128)S(1)} %copy.5), channel_id=1, source_target_pairs={{0,8},{8,16},{16,24},{24,32},{32,40},{40,48},{48,56},{56,64},{64,7... | collective-permute-start | bytes 518408 | tf_op jit(solution)/shard_map/ppermute | solution.py:26
  56.1 11.8 %collective-permute-start.11 = (f32[6,100,36,2]{1,3,2,0:T(2,128)S(1)}, f32[6,100,36,2]{1,3,2,0:T(2,128)S(1)}, u32[]{:S(2)}, u32[]{:S(2)}) collective-permute-start(f32[6,100,36,2]{1,3,2,0:T(2,128)S(1)} %copy.6), channel_id=1, source_target_pairs={{8,0},{16,8},{24,16},{32,24},{40,32},{48,40},{56,48},{64,56},{72,6... | collective-permute-start | bytes 518408 | tf_op jit(solution)/shard_map/ppermute | solution.py:29
  201.7 7.3 collective-permute-start.3
  213.6 7.1 collective-permute-start.6
  213.6 7.1 collective-permute-start.7
  230.5 7.3 collective-permute-start.3
  242.4 7.1 collective-permute-start.6
  242.4 7.1 collective-permute-start.7
  259.3 7.3 collective-permute-start.3
  271.2 7.1 collective-permute-start.6
  271.2 7.1 collective-permute-start.7
  288.1 7.3 collective-permute-start.3
  299.9 7.1 collective-permute-start.6
  300.0 7.1 collective-permute-start.7
  316.9 7.3 collective-permute-start.3
  328.7 7.1 collective-permute-start.6
  328.8 7.1 collective-permute-start.7
  345.7 7.3 collective-permute-start.3
  357.5 7.1 collective-permute-start.6
  357.6 7.1 collective-permute-start.7
  374.5 7.3 collective-permute-start.3
  386.3 7.1 collective-permute-start.6
  386.4 7.1 collective-permute-start.7
  403.3 7.3 collective-permute-start.3
  415.1 7.1 collective-permute-start.6
  415.2 7.1 collective-permute-start.7
  432.1 7.3 collective-permute-start.3
  443.9 7.1 collective-permute-start.6
  444.0 7.1 collective-permute-start.7
  460.9 7.3 collective-permute-start.3
  472.7 7.1 collective-permute-start.6
  489.7 7.3 collective-permute-start.3
  501.5 7.1 collective-permute-start.6
  518.5 7.3 collective-permute-start.3
  530.3 7.1 collective-permute-start.6
  547.3 7.3 collective-permute-start.3
  559.1 7.1 collective-permute-start.6
  576.1 7.3 collective-permute-start.3
  587.9 7.1 collective-permute-start.6
  587.9 7.1 collective-permute-start.7
  604.8 7.3 collective-permute-start.3
  616.7 7.1 collective-permute-start.6
  633.6 7.3 collective-permute-start.3
  645.5 7.1 collective-permute-start.6
  672.4 10.0 %collective-permute-start.14 = (f32[2,100,34,1]{1,0,3,2:T(2,128)S(1)}, f32[2,100,34,1]{1,0,3,2:T(2,128)}, u32[]{:S(2)}, u32[]{:S(2)}) collective-permute-start(f32[2,100,34,1]{1,0,3,2:T(2,128)S(1)} %copy.9), channel_id=1, source_target_pairs={{0,8},{8,16},{16,24},{24,32},{32,40},{40,48},{48,56},{56,64},{64,7... | collective-permute-start | bytes 81608 | tf_op jit(solution)/shard_map/ppermute | solution.py:26
  676.5 9.9 %collective-permute-start.15 = (f32[2,100,34,1]{1,0,3,2:T(2,128)}, f32[2,100,34,1]{1,0,3,2:T(2,128)}, u32[]{:S(2)}, u32[]{:S(2)}) collective-permute-start(f32[2,100,34,1]{1,0,3,2:T(2,128)} %copy.10), channel_id=1, source_target_pairs={{8,0},{16,8},{24,16},{32,24},{40,32},{48,40},{56,48},{64,56},{72,6... | collective-permute-start | bytes 81608 | tf_op jit(solution)/shard_map/ppermute | solution.py:29
  (110 other events, 632.2 us)
where the time goes:
time: 779 us; the launch traced here: 771 us
  waiting for transfers between devices  272 us (35%)
  other arithmetic  210 us (27%)
  starting transfers between devices  205 us (26%)
  local copies, waits for them, and re-layouts  80.6 us (10%)
    ppermute x68, waiting for transfers between devices, extended(): lax.ppermute(lax.slice_in_dim(block, block.shape[dim] - width, None, axis...  219 us
    ppermute x68, starting transfers between devices, extended(): lax.ppermute(lax.slice_in_dim(block, 0, width, axis=dim), axis, backward)  188 us
    ppermute x68, waiting for transfers between devices, extended(): lax.ppermute(lax.slice_in_dim(block, 0, width, axis=dim), axis, backward)  52.7 us
    concatenate x52, other arithmetic, extended(): block = jnp.concatenate([low, block, high], axis=dim)  43.9 us
    another operation x1, other arithmetic, pressure(): return jnp.cumsum(weight, axis=0) - 0.5 * weight  37 us
    mul x1, other arithmetic, transport(): (thick * tracer - time_step * (east_diff(flux_east * tracer_wide) + north...  22.5 us
    another operation x1, other arithmetic, baroclinic(): tendency = jnp.stack([tend_east, tend_north])  22.5 us
    slice x19, local copies, waits for them, and re-layouts, extended(): lax.slice_in_dim(block, 0, width, axis=dim)  22.4 us
  transfers between devices with their start and end apart: 136, of which 113 were waited for; matrix products, arithmetic and copies ran while one was open for 3% of the time, Pallas kernels for 0%

commit v1 on v0

v1 whole, which is shorter than its diff:
```python
import jax
import jax.numpy as jnp
from jax import lax
from jax.experimental import pallas as pl
from jax.experimental.pallas import tpu as pltpu
from jax.sharding import PartitionSpec as P

K = 100
NSUB = 16
R = 32
C = 128
CH = 25
NY = 256

DT = 0.1
TAU = 0.6
NU = 0.01
KAPPA = 0.1
GRAV = 0.1
THERMAL = 1.0
HALINE = 0.8
ROT = 0.5

F32 = jnp.float32
MESH = pl.DeviceIdType.MESH


def lanes(shape=(1, C)):
    return lax.broadcasted_iota(jnp.int32, shape, 1)


def sublanes(shape):
    return lax.broadcasted_iota(jnp.int32, shape, 0)


def roll(x, s):
    if isinstance(s, int):
        s %= C
        if s == 0:
            return x
    return pltpu.roll(x, s, axis=1)


def kernel_a(
    layers, kmt_ref, baro_ref,
    q_out, a2d_out, baro_out, col_out, row_out,
    uv, s, p, q, cuv, cs,
    m_uv, r_uv, m_p, r_p, m_s, r_s, m_q, r_q,
    d4, corr,
    b1, m1, r1, b2, m2, r2, a0v, r_a0v, r_rows, r_qrows,
    eta, ua, vv, dvv, da, dv, c2, c2a, cfa, cfv, sa, sv,
    load_sem, out_sem, send_sem, recv_sem,
):
    lon = lax.axis_index("lon")
    lat = lax.axis_index("lat")
    nlon = lax.axis_size("lon")
    nlat = lax.axis_size("lat")
    east = lax.rem(lon + 1, nlon)
    west = lax.rem(lon + nlon - 1, nlon)
    north = lax.rem(lat + 1, nlat)
    south = lax.rem(lat + nlat - 1, nlat)
    x_of = {-1: west, 0: lon, 1: east}
    y_of = {-1: south, 0: lat, 1: north}

    loads = {}
    n_load = 0
    for f in range(2):
        cp = pltpu.make_async_copy(layers.at[f], uv.at[f, :, 8:40, :], load_sem.at[n_load])
        cp.start()
        loads["uv", f] = cp
        n_load += 1
    for c in range(4):
        cp = pltpu.make_async_copy(
            layers.at[2:5, c * CH:(c + 1) * CH], s.at[0:3, c * CH:(c + 1) * CH], load_sem.at[n_load])
        cp.start()
        loads["s", c] = cp
        n_load += 1
    cp = pltpu.make_async_copy(layers.at[5], s.at[3], load_sem.at[n_load])
    cp.start()
    loads["age"] = cp

    barrier = pltpu.get_barrier_semaphore()
    around = [(dx, dy) for dx in (-1, 0, 1) for dy in (-1, 0, 1) if (dx, dy) != (0, 0)]
    for dx, dy in around:
        pl.semaphore_signal(barrier, inc=1, device_id=(x_of[dx], y_of[dy]), device_id_type=MESH)

    copies = {}

    def send(name, src, dst, dx, dy):
        at = len(copies)
        cp = pltpu.make_async_remote_copy(
            src_ref=src, dst_ref=dst, send_sem=send_sem.at[at], recv_sem=recv_sem.at[at],
            device_id=(x_of[dx], y_of[dy]), device_id_type=MESH)
        cp.start()
        copies[name] = cp

    lane = lanes()
    quad = lane >> 2
    in_quad = lane & 3
    kmt = kmt_ref[...]
    cmask = (kmt > 0).astype(F32)

    b1[1, 40:72, :] = baro_ref[1] * cmask
    b1[2, 40:72, :] = baro_ref[2] * cmask
    b1[3, 40:72, :] = kmt.astype(F32)

    for f in range(2):
        loads["uv", f].wait()

        def body(j, acc, f=f):
            xs = []
            for c in range(4):
                k = c * CH + j
                xs.append(jnp.where(k < kmt, uv[f, k, 8:40, :], 0.0))
            sel = quad == j
            out = []
            for c in range(4):
                out.append(jnp.where(sel, roll(xs[c], 4 * j + 2), acc[c]))
            for c in range(4):
                uv[f, c * CH + j, 8:40, :] = xs[c]
            return tuple(out)

        zero = jnp.zeros((R, C), F32)
        acc = lax.fori_loop(0, CH, body, (zero,) * 4)
        for c in range(4):
            cuv[f, c, 8:40, :] = acc[c]

    for c in range(4):
        cu, cv = cuv[0, c, 8:40, :], cuv[1, c, 8:40, :]
        m_uv[0, c] = jnp.where(in_quad < 2, cu, roll(cv, 2))
        m_uv[1, c] = jnp.where(in_quad < 2, roll(cu, -2), cv)

    pl.semaphore_wait(barrier, 8)

    send("uv_n", uv.at[:, :, 38:40, :], uv.at[:, :, 6:8, :], 0, 1)
    send("uv_s", uv.at[:, :, 8:10, :], uv.at[:, :, 40:42, :], 0, -1)
    for d, dx in ((0, 1), (1, -1)):
        send(("uv", dx, 0), m_uv.at[d], r_uv.at[d, :, 8:40, :], dx, 0)
        send(("uv", dx, 1), m_uv.at[d, :, 24:32, :], r_uv.at[d, :, 0:8, :], dx, 1)
        send(("uv", dx, -1), m_uv.at[d, :, 0:8, :], r_uv.at[d, :, 40:48, :], dx, -1)
    send("cuv_n", cuv.at[:, :, 32:40, :], cuv.at[:, :, 0:8, :], 0, 1)
    send("cuv_s", cuv.at[:, :, 8:16, :], cuv.at[:, :, 40:48, :], 0, -1)

    zero = jnp.zeros((R, C), F32)
    csum, total = zero, zero
    for c in range(4):
        loads["s", c].wait()

        def body(j, carry, c=c):
            csum, total, acc = carry
            k = c * CH + j
            m = k < kmt
            h = jnp.where(m, s[0, k], 0.0)
            w = ((GRAV * HALINE) * s[2, k] - (GRAV * THERMAL) * s[1, k]) * h
            pk = csum + 0.5 * w
            p[k, 8:40, :] = pk
            acc = jnp.where(quad == j, roll(pk, 4 * j + 2), acc)
            return csum + w, total + h, acc

        csum, total, acc = lax.fori_loop(0, CH, body, (csum, total, zero))
        cs[0, c] = acc

    def compact(field, lane_from):
        out = roll(cs[field, 0], -lane_from)
        for c in range(1, 4):
            out = jnp.where(in_quad == c, roll(cs[field, c], c - lane_from), out)
        return out

    m_p[0] = compact(0, 1)
    m_p[1] = compact(0, 2)
    b1[0, 40:72, :] = total * (1.0 / K)

    def side(fields, eastward):
        out = None
        for n, x in enumerate(fields):
            moved = roll(x, 32 * n + 32) if eastward else roll(x, 32 * n)
            out = moved if out is None else jnp.where(lane < 32 * n, out, moved)
        return out

    def unside(n, d):
        return (roll(d[0], 96 - 32 * n), roll(d[1], -32 * n))

    mine = [b1[n, 40:72, :] for n in range(3)]
    m1[0] = side(mine, True)
    m1[1] = side(mine, False)

    def send_sides(tag, m, r):
        for d, dx in ((0, 1), (1, -1)):
            send((tag, dx, 0), m.at[d], r.at[d, 32:64, :], dx, 0)
            send((tag, dx, 1), m.at[d], r.at[d, 0:32, :], dx, 1)
            send((tag, dx, -1), m.at[d], r.at[d, 64:96, :], dx, -1)

    send("p_e", m_p.at[0], r_p.at[0], 1, 0)
    send("p_w", m_p.at[1], r_p.at[1], -1, 0)
    send("p_n", p.at[:, 39, :], p.at[:, 7, :], 0, 1)
    send("p_s", p.at[:, 8, :], p.at[:, 40, :], 0, -1)
    send("b1_n", b1.at[:, 40:72, :], b1.at[:, 8:40, :], 0, 1)
    send("b1_s", b1.at[:, 40:72, :], b1.at[:, 72:104, :], 0, -1)
    send_sides("b1", m1, r1)

    loads["age"].wait()
    for f in range(4):

        def body(j, acc, f=f):
            sel = quad == j
            out = []
            for c in range(4):
                k = c * CH + j
                x = jnp.where(k < kmt, s[f, k], 0.0)
                out.append(jnp.where(sel, roll(x, 4 * j + 2), acc[c]))
            return tuple(out)

        acc = lax.fori_loop(0, CH, body, (zero,) * 4)
        for c in range(4):
            cs[1 + f, c] = acc[c]
        m_s[0, f] = compact(1 + f, 1)
        m_s[1, f] = compact(1 + f, 2)
    send("s_e", m_s.at[0], r_s.at[0], 1, 0)
    send("s_w", m_s.at[1], r_s.at[1], -1, 0)
    send("s_n", s.at[:, :, 31, :], r_rows.at[0], 0, 1)
    send("s_s", s.at[:, :, 0, :], r_rows.at[1], 0, -1)

    for name in ("b1_n", "b1_s"):
        copies[name].wait_recv()
    for dx in (1, -1):
        for dy in (0, 1, -1):
            copies["b1", dx, dy].wait_recv()
    for ref in (eta, dvv):
        for t in range(2):
            ref[t, 0:8, :] = jnp.zeros((8, C), F32)
            ref[t, 104:112, :] = jnp.zeros((8, C), F32)

    def tiles_of(n, centre, r, at):
        lo, hi = at
        t0 = centre[n, 8 + lo:8 + hi, :]
        from_west, from_east = unside(n, (r[0, lo:hi, :], r[1, lo:hi, :]))
        t1 = jnp.where(lane < 32, from_east, jnp.where(lane >= 96, from_west, 0.0))
        return t0, t1

    def shift_west(t0, t1):
        a, b = roll(t0, 1), roll(t1, 1)
        return jnp.where(lane < 1, b, a), jnp.where(lane < 1, a, b)

    for blk in range(3):
        at = (32 * blk, 32 * blk + 32)
        here = slice(8 + 32 * blk, 40 + 32 * blk)
        dd = tiles_of(0, b1, r1, at)
        uu = tiles_of(1, b1, r1, at)
        ww = tiles_of(2, b1, r1, at)
        dda = shift_west(*dd)
        uua = shift_west(*uu)
        for t in range(2):
            da[t, here, :] = dda[t]
            ua[t, here, :] = uua[t]
            dv[t, here, :] = dd[t]
            vv[t, here, :] = ww[t]
            dvv[t, here, :] = dd[t] * ww[t]
            c2[t, here, :] = jnp.where(dd[t] > 0.0, 0.5 * TAU, 0.0)
            c2a[t, here, :] = jnp.where(dda[t] > 0.0, 0.5 * TAU, 0.0)

    def next_height(lo, both):
        n = 2 if both else 1
        at = pl.ds(lo, 8)
        x = [da[t, at, :] * ua[t, at, :] for t in range(2)]
        r = [roll(x[t], -2) for t in range(2)]
        out = []
        for t in range(n):
            diff = jnp.where(lane < 126, r[t], r[1 - t]) - x[t]
            diff = diff + (dvv[t, pl.ds(lo + 1, 8), :] - dvv[t, pl.ds(lo - 1, 8), :])
            out.append(c2[t, at, :] * diff)
        return out

    for i in range(4):
        drop = next_height(40 + 8 * i, False)[0]
        b2[2, 40 + 8 * i:48 + 8 * i, :] = (
            baro_ref[0, 8 * i:8 * i + 8, :] * cmask[8 * i:8 * i + 8] - drop)

    for name in ("cuv_n", "cuv_s"):
        copies[name].wait_recv()
    for dx in (1, -1):
        for dy in (0, 1, -1):
            copies["uv", dx, dy].wait_recv()
    for c in range(4):
        w, e = r_uv[0, c], r_uv[1, c]
        d4[0, c] = jnp.where(in_quad < 2, w, roll(e, 2)) - cuv[0, c]
        d4[1, c] = jnp.where(in_quad < 2, roll(w, -2), e) - cuv[1, c]
    copies["p_e"].wait_recv()
    copies["p_w"].wait_recv()
    p_w, p_e = r_p[0], r_p[1]
    for c in range(4):
        for f in range(2):
            x = d4[f, c, 8:40, :]
            g = 2.0 * (d4[f, c, 9:41, :] + d4[f, c, 7:39, :]) - 8.0 * x
            out = jnp.where(in_quad < 2, roll(x, -2), roll(x, 2))
            out = out + jnp.where(in_quad == 1, roll(g, -1), jnp.where(in_quad == 2, roll(g, 1), 0.0))
            out = -NU * out
            if f == 0:
                own = cs[0, c]
                at_127 = 0.5 * (roll(own, -1) - roll(p_e, 1 - c))
                at_0 = 0.5 * (roll(p_w, 2 - c) - roll(own, 1))
                out = out + jnp.where(in_quad == 1, at_127, jnp.where(in_quad == 2, at_0, 0.0))
            corr[f, c] = out

    for name in ("uv_n", "uv_s", "p_n", "p_s"):
        copies[name].wait_recv()

    row = sublanes((R, C)) + lat * R
    cor = ROT * (2.0 * (row.astype(F32) + 0.5) / NY - 1.0)
    edge4 = (lane >= 126) | (lane < 2)

    def bilaplace(f, k):
        x = uv[f, k, 8:40, :]
        a = uv[f, k, 9:41, :] + uv[f, k, 7:39, :]
        b = uv[f, k, 10:42, :] + uv[f, k, 6:38, :]
        t = 2.0 * a - 8.0 * x
        e = roll(roll(x, -1) + t, -1)
        w = roll(roll(x, 1) + t, 1)
        return x, e + w + (b - 4.0 * t - 12.0 * x)

    sums = (zero,) * 4
    for c in range(4):

        def body(j, carry, c=c):
            sgu, sgv, squ, sqv, acc = carry
            k = c * CH + j
            m = k < kmt
            u0, lu = bilaplace(0, k)
            v0, lv = bilaplace(1, k)
            pk = p[k, 8:40, :]
            back = lax.rem(126 + C - 4 * j, C)
            cu = jnp.where(edge4, roll(corr[0, c], back), 0.0)
            cv = jnp.where(edge4, roll(corr[1, c], back), 0.0)
            gu = cor * v0 - NU * lu - 0.5 * (roll(pk, -1) - roll(pk, 1)) + cu
            gv = cv - cor * u0 - NU * lv - 0.5 * (p[k, 9:41, :] - p[k, 7:39, :])
            gu = jnp.where(m, gu, 0.0)
            gv = jnp.where(m, gv, 0.0)
            qu = u0 + DT * gu
            qv = v0 + DT * gv
            q[0, k] = qu
            q[1, k] = qv
            h = s[0, k]
            acc = jnp.where(quad == j, roll(qu, 4 * j + 2), acc)
            return sgu + gu * h, sgv + gv * h, squ + qu * h, sqv + qv * h, acc

        *sums, acc = lax.fori_loop(0, CH, body, (*sums, zero))
        cs[0, c] = acc
    sgu, sgv, squ, sqv = sums

    out_copies = []
    for f in range(2):
        cp = pltpu.make_async_copy(q.at[f], q_out.at[f], out_sem.at[f])
        cp.start()
        out_copies.append(cp)

    bound = jnp.maximum(total, 1.0)
    fu, fv = sgu / bound, sgv / bound
    a0u = -DT * fu - (squ - DT * fu * total) / bound
    a0v[...] = -DT * fv - (sqv - DT * fv * total) / bound
    b2[0, 40:72, :] = fu
    b2[1, 40:72, :] = fv
    mine = [fu, fv, b2[2, 40:72, :], a0u]
    m2[0] = side(mine, True)
    m2[1] = side(mine, False)
    send("b2_n", b2.at[:, 40:72, :], b2.at[:, 8:40, :], 0, 1)
    send("b2_s", b2.at[:, 40:72, :], b2.at[:, 72:104, :], 0, -1)
    send_sides("b2", m2, r2)
    send("a_n", a0v.at[24:32, :], r_a0v.at[0], 0, 1)
    send("a_s", a0v.at[0:8, :], r_a0v.at[1], 0, -1)
    m_q[0] = compact(0, 1)
    m_q[1] = compact(0, 2)
    send("q_e", m_q.at[0], r_q.at[0], 1, 0)
    send("q_w", m_q.at[1], r_q.at[1], -1, 0)
    send("q_n", q.at[1, :, 31, :], r_qrows.at[0], 0, 1)
    send("q_s", q.at[1, :, 0, :], r_qrows.at[1], 0, -1)

    for name in ("b2_n", "b2_s"):
        copies[name].wait_recv()
    for dx in (1, -1):
        for dy in (0, 1, -1):
            copies["b2", dx, dy].wait_recv()
    for blk in range(3):
        at = (32 * blk, 32 * blk + 32)
        here = slice(8 + 32 * blk, 40 + 32 * blk)
        ffu = shift_west(*tiles_of(0, b2, r2, at))
        ffv = tiles_of(1, b2, r2, at)
        ee = tiles_of(2, b2, r2, at)
        for t in range(2):
            eta[t, here, :] = ee[t]
            cfa[t, here, :] = 2.0 * c2a[t, here, :] * ffu[t]
            cfv[t, here, :] = 2.0 * c2[t, here, :] * ffv[t]

    sa[...] = jnp.zeros((2, R, C), F32)
    sv[...] = jnp.zeros((48, C), F32)

    def flows(first, count):
        for i in range(count):
            lo = 8 + 8 * (first + i)
            at = slice(lo, lo + 8)
            e = [eta[t, at, :] for t in range(2)]
            r = [roll(e[t], 2) for t in range(2)]
            for t in range(2):
                diff = e[t] - jnp.where(lane < 2, r[1 - t], r[t])
                new_u = ua[t, at, :] + (cfa[t, at, :] - c2a[t, at, :] * diff)
                ua[t, at, :] = new_u
                diff = eta[t, lo + 1:lo + 9, :] - eta[t, lo - 1:lo + 7, :]
                new_v = vv[t, at, :] + (cfv[t, at, :] - c2[t, at, :] * diff)
                vv[t, at, :] = new_v
                dvv[t, at, :] = dv[t, at, :] * new_v
                if 40 <= lo < 72:
                    sa[t, lo - 40:lo - 32, :] += new_u
                if t == 0 and 32 <= lo < 80:
                    sv[lo - 32:lo - 24, :] += new_v

    def heights(first, count):
        for i in range(count):
            lo = 8 + 8 * (first + i)
            drop = next_height(lo, True)
            for t in range(2):
                eta[t, lo:lo + 8, :] = eta[t, lo:lo + 8, :] - drop[t]

    flows(0, 12)
    for group in range(4):
        first, count = group, 12 - 2 * group

        def body(n, carry, first=first, count=count):
            heights(first, count)
            flows(first, count)
            return carry

        lax.fori_loop(0, 3 if group == 0 else 4, body, 0)

    sa0, sa1 = sa[0], sa[1]
    su = jnp.where(lane < 127, roll(sa0, -1), roll(sa1, -1))
    a2d_out[0] = a0u + su * (1.0 / NSUB)
    a2d_out[1] = a0v[...] + sv[8:40, :] * (1.0 / NSUB)
    baro_out[0] = eta[0, 40:72, :]
    baro_out[1] = jnp.where(lane < 127, roll(ua[0, 40:72, :], -1), roll(ua[1, 40:72, :], -1))
    baro_out[2] = vv[0, 40:72, :]

    for name in ("s_e", "s_w", "q_e", "q_w"):
        copies[name].wait_recv()
    a_w = r2[0, 32:64, 127:128] + sa0[:, 0:1] * (1.0 / NSUB)
    a_e = r2[1, 32:64, 96:97] + sa1[:, 1:2] * (1.0 / NSUB)
    halves = []
    for d, a, sign in ((0, a_w, 1.0), (1, a_e, -1.0)):
        flux = (0.5 * DT) * r_s[d, 0] * (r_q[d] + a)
        vals = [flux]
        for n in range(1, 4):
            vals.append(r_s[d, n] * ((DT * KAPPA) + sign * flux))
        halves.append(vals)
    for n in range(4):
        w, e = halves[0][n], halves[1][n]
        col_out[n, 0] = jnp.where(
            in_quad == 0, e, jnp.where(in_quad == 1, roll(w, 1), jnp.where(in_quad == 2, roll(e, 1), roll(w, 2))))
        col_out[n, 1] = jnp.where(
            in_quad == 0, roll(e, -2), jnp.where(in_quad == 1, roll(w, -1), jnp.where(in_quad == 2, roll(e, -1), w)))

    for name in ("s_n", "s_s", "q_n", "q_s", "a_n", "a_s"):
        copies[name].wait_recv()
    level = sublanes((K, C)).astype(F32)
    for d, kmt_row, a_row, sign in (
        (0, b1[3, 39:40, :], r_a0v[0, 7:8, :] + sv[7:8, :] * (1.0 / NSUB), 1.0),
        (1, b1[3, 72:73, :], r_a0v[1, 0:1, :] + sv[40:41, :] * (1.0 / NSUB), -1.0),
    ):
        m = level < kmt_row
        flux = jnp.where(m, (0.5 * DT) * r_rows[d, 0] * (r_qrows[d] + a_row), 0.0)
        row_out[4 * d] = flux
        for n in range(1, 4):
            row_out[4 * d + n] = jnp.where(m, r_rows[d, n], 0.0) * ((DT * KAPPA) + sign * flux)

    for cp in copies.values():
        cp.wait_send()
    for cp in out_copies:
        cp.wait()


N_COPIES = 2 + 6 + 2 + 4 + 2 + 6 + 4 + 2 + 6 + 2 + 4


def call_a(layers, kmt, baro):
    v = lambda *shape: pltpu.VMEM(shape, F32)
    surface = [v(2, 112, C) for _ in range(10)]
    return pl.pallas_call(
        kernel_a,
        out_shape=(
            jax.ShapeDtypeStruct((2, K, R, C), F32),
            jax.ShapeDtypeStruct((2, R, C), F32),
            jax.ShapeDtypeStruct((3, R, C), F32),
            jax.ShapeDtypeStruct((4, 2, R, C), F32),
            jax.ShapeDtypeStruct((8, K, C), F32),
        ),
        in_specs=[
            pl.BlockSpec(memory_space=pl.ANY),
            pl.BlockSpec(memory_space=pltpu.VMEM),
            pl.BlockSpec(memory_space=pltpu.VMEM),
        ],
        out_specs=(
            pl.BlockSpec(memory_space=pl.ANY),
            pl.BlockSpec(memory_space=pltpu.VMEM),
            pl.BlockSpec(memory_space=pltpu.VMEM),
            pl.BlockSpec(memory_space=pltpu.VMEM),
            pl.BlockSpec(memory_space=pltpu.VMEM),
        ),
        scratch_shapes=[
            v(2, K, 48, C), v(4, K, R, C), v(K, 48, C), v(2, K, R, C), v(2, 4, 48, C), v(5, 4, R, C),
            v(2, 4, R, C), v(2, 4, 48, C), v(2, R, C), v(2, R, C), v(2, 4, R, C), v(2, 4, R, C), v(2, R, C), v(2, R, C),
            v(2, 4, 48, C), v(2, 4, R, C),
            v(4, 112, C), v(2, R, C), v(2, 96, C), v(3, 112, C), v(2, R, C), v(2, 96, C),
            v(R, C), v(2, 8, C), v(2, 4, K, C), v(2, K, C),
            *surface, v(2, R, C), v(48, C),
            pltpu.SemaphoreType.DMA((7,)),
            pltpu.SemaphoreType.DMA((2,)),
            pltpu.SemaphoreType.DMA((N_COPIES,)),
            pltpu.SemaphoreType.DMA((N_COPIES,)),
        ],
        compiler_params=pltpu.CompilerParams(
            collective_id=0, has_side_effects=True, vmem_limit_bytes=50 * 2**20),
        name="tendencies_and_surface",
    )(layers, kmt, baro)


LB = 10


def kernel_b(ht, sa, q, a2d, kmt_ref, col, rows, baro, out, baro_out):
    step = pl.program_id(0)
    lane = lanes()
    sub = sublanes((8, C))
    kmt = kmt_ref[...]
    au, av = a2d[0], a2d[1]
    kd = DT * KAPPA

    @pl.when(step == 0)
    def _():
        baro_out[...] = baro[...]

    def tiles(x):
        return [x[8 * i:8 * i + 8] for i in range(4)]

    def from_north(x, halo):
        r = [pltpu.roll(t, 7, axis=0) for t in tiles(x)] + [jnp.broadcast_to(halo, (8, C))]
        return jnp.concatenate([jnp.where(sub == 7, r[i + 1], r[i]) for i in range(4)], axis=0)

    def from_south(x, halo):
        r = [jnp.broadcast_to(halo, (8, C))] + [pltpu.roll(t, 1, axis=0) for t in tiles(x)]
        return jnp.concatenate([jnp.where(sub == 0, r[i], r[i + 1]) for i in range(4)], axis=0)

    def body(l, carry):
        k = step * LB + l
        c = k // CH
        j = k - c * CH
        tile = k // (2 * CH)
        back = 127 - 4 * j - 2 * (c - 2 * tile)
        m = k < kmt
        h = ht[0, l]
        un = jnp.where(m, q[0, l] + au, 0.0)
        vn = jnp.where(m, q[1, l] + av, 0.0)
        out[0, l] = un
        out[1, l] = vn
        h5 = (0.5 * DT) * h
        fu, fv = h5 * un, h5 * vn

        def halo(n):
            return roll(col[n, tile], back)

        def row_n(n):
            return rows[4 + n, pl.ds(k, 1), :]

        def row_s(n):
            return rows[n, pl.ds(k, 1), :]

        hal = halo(0)
        e = jnp.where(lane == 127, hal, roll(fu, -1))
        w = jnp.where(lane == 0, hal, roll(fu, 1))
        hn = h - ((e - w) + (from_north(fv, row_n(0)) - from_south(fv, row_s(0))))
        out[2, l] = jnp.where(m, hn, 0.0)
        ke, kw, kn, ks = kd - fu, kd + fu, kd - fv, kd + fv
        mid = h - 4.0 * kd
        for n, (ref, at) in enumerate(((ht, 1), (sa, 0), (sa, 1)), start=1):
            x = jnp.where(m, ref[at, l], 0.0)
            hal = halo(n)
            e = jnp.where(lane == 127, hal, roll(x * ke, -1))
            w = jnp.where(lane == 0, hal, roll(x * kw, 1))
            r = from_north(x * kn, row_n(n)) + from_south(x * ks, row_s(n))
            out[2 + n, l] = jnp.where(m, (e + w) + (r + x * mid), 0.0)
        return carry

    lax.fori_loop(0, LB, body, 0)


def call_b(layers, q, a2d, kmt, col, rows, baro):
    whole = lambda *shape: pl.BlockSpec(shape, lambda i: (0,) * len(shape))
    return pl.pallas_call(
        kernel_b,
        grid=(K // LB,),
        out_shape=(
            jax.ShapeDtypeStruct((6, K, R, C), F32),
            jax.ShapeDtypeStruct((3, R, C), F32),
        ),
        in_specs=[
            pl.BlockSpec((2, LB, R, C), lambda i: (1, i, 0, 0)),
            pl.BlockSpec((2, LB, R, C), lambda i: (2, i, 0, 0)),
            pl.BlockSpec((2, LB, R, C), lambda i: (0, i, 0, 0)),
            whole(2, R, C), whole(R, C), whole(4, 2, R, C), whole(8, K, C), whole(3, R, C),
        ],
        out_specs=(
            pl.BlockSpec((6, LB, R, C), lambda i: (0, i, 0, 0)),
            whole(3, R, C),
        ),
        compiler_params=pltpu.CompilerParams(vmem_limit_bytes=40 * 2**20),
        name="transport",
    )(layers, layers, q, a2d, kmt, col, rows, baro)


def per_device(layers, kmt, barotropic):
    q, a2d, baro, col, rows = call_a(layers, kmt, barotropic)
    return call_b(layers, q, a2d, kmt, col, rows, baro)


def solution(mesh):
    return jax.shard_map(
        per_device,
        mesh=mesh,
        in_specs=(P(None, None, "lat", "lon"), P("lat", "lon"), P(None, "lat", "lon")),
        out_specs=(P(None, None, "lat", "lon"), P(None, "lat", "lon")),
        check_vma=False,
    )
```

time: 779 us -> 83.2 us (0.11)
  waiting for transfers between devices: 272 us -> 0 us
  other arithmetic: 210 us -> 0 us
  starting transfers between devices: 205 us -> 0 us
  Pallas kernels: 0 us -> 76.3 us
  local copies, waits for them, and re-layouts: 80.6 us -> 5.44 us
    ppermute x136 -> x0, waiting for transfers between devices: 272 us -> none  [the longest x68 219 us: extended(): lax.ppermute(lax.slice_in_dim(block, block.shape[dim] - width, None, axis...]
    ppermute x136 -> x0, starting transfers between devices: 205 us -> none  [the longest x68 188 us: extended(): lax.ppermute(lax.slice_in_dim(block, 0, width, axis=dim), axis, backward)]
    pallas_call x0 -> x2, Pallas kernels: none -> 76.3 us  [the longest x1 61.6 us: call_a(): pl.pallas_call(kernel_a, out_shape=(jax.ShapeDtypeStruct((2, K, R, C), F3...]
    mul x24 -> x0, other arithmetic: 65.2 us -> none  [the longest x1 22.5 us: transport(): (thick * tracer - time_step * (east_diff(flux_east * tracer_wide) + north...]
    another operation x19 -> x0, other arithmetic: 60.2 us -> none  [the longest x1 37 us: pressure(): return jnp.cumsum(weight, axis=0) - 0.5 * weight]
    concatenate x53 -> x0, other arithmetic: 53.9 us -> none  [the longest x52 43.9 us: extended(): block = jnp.concatenate([low, block, high], axis=dim)]
    slice x56 -> x0, local copies, waits for them, and re-layouts: 39.9 us -> none  [the longest x19 22.4 us: extended(): lax.slice_in_dim(block, 0, width, axis=dim)]
    ppermute x4 -> x0, local copies, waits for them, and re-layouts: 22.1 us -> none  [the longest x2 11.1 us: extended(): lax.ppermute(lax.slice_in_dim(block, block.shape[dim] - width, None, axis...]
  transfers between devices with their start and end apart: 136 -> 0, of which waited for: 113 -> 0; matrix products, arithmetic and copies ran while one was open for 3% -> 0% of each run, Pallas kernels for 0% -> 0%
where the time goes in v1:
time: 83.2 us; the launch traced here: 82.4 us
  Pallas kernels  76.3 us (92%)
  local copies, waits for them, and re-layouts  5.44 us (7%)
    pallas_call x1, Pallas kernels, call_a(): pl.pallas_call(kernel_a, out_shape=(jax.ShapeDtypeStruct((2, K, R, C), F3...  61.6 us
    pallas_call x1, Pallas kernels, call_b(): pl.pallas_call(kernel_b, grid=(K // LB,), out_shape=(jax.ShapeDtypeStruct...  14.7 us
    unnamed x12, local copies, waits for them, and re-layouts  5.44 us

profile of v1, /device:TPU:0, one launch (start us, length us, event | category | flops | bytes accessed | tf_op | source)
XLA Modules:
  0.0 82.4 jit_solution(7760036818855644600)
XLA Ops:
  0.6 0.0 copy-start
  0.6 0.0 copy-start.3
  0.6 0.9 %copy-done.3 = s32[32,128]{1,0:T(8,128)S(1)} copy-done((s32[32,128]{1,0:T(8,128)S(1)}, s32[32,128]{1,0:T(8,128)}, u32[]{:S(2)}) %copy-start.3) | copy-done | bytes 16408
  1.5 0.0 copy-start.5
  1.5 0.9 %copy-done.5 = f32[3,32,128]{2,1,0:T(8,128)S(1)} copy-done((f32[3,32,128]{2,1,0:T(8,128)S(1)}, f32[3,32,128]{2,1,0:T(8,128)}, u32[]{:S(2)}) %copy-start.5) | copy-done | bytes 49176
  2.5 0.0 copy-start.4
  2.5 61.6 %tendencies_and_surface.1 = (f32[2,100,32,128]{3,2,1,0:T(8,128)S(1)}, f32[2,32,128]{2,1,0:T(8,128)S(1)}, f32[3,32,128]{2,1,0:T(8,128)S(1)}, f32[4,2,32,128]{3,2,1,0:T(8,128)S(1)}, f32[8,100,128]{2,1,0:T(8,128)S(1)}) custom-call(f32[6,100,32,128]{3,2,1,0:T(8,128)} %sa.1, s32[32,128]{1,0:T(8,128)S(1)} %copy-done.3, f32[3,32,128]{2,1,0:T(8,128)S(1)} %copy-done.5), custom_call_target="tpu_custom_call" | custom-call | tf_op jit(solution)/shard_map/tendencies_and_surface/pallas_call | solution.py:483
  64.1 0.0 copy-start.1
  64.1 1.7 %copy-done.1 = f32[2,100,32,128]{3,2,1,0:T(8,128)} copy-done((f32[2,100,32,128]{3,2,1,0:T(8,128)}, f32[2,100,32,128]{3,2,1,0:T(8,128)S(1)}, u32[]{:S(2)}) %copy-start.1) | copy-done | bytes 3276824
  65.8 0.0 copy-done
  65.8 0.0 copy-done.4
  65.8 0.0 copy-start.2
  65.8 1.9 %copy-done.2 = f32[2,100,32,128]{3,2,1,0:T(8,128)S(1)} copy-done((f32[2,100,32,128]{3,2,1,0:T(8,128)S(1)}, f32[2,100,32,128]{3,2,1,0:T(8,128)}, u32[]{:S(2)}) %copy-start.2) | copy-done | bytes 3276824
  67.7 14.7 %transport.1 = (f32[6,100,32,128]{3,2,1,0:T(8,128)}, f32[3,32,128]{2,1,0:T(8,128)}) custom-call(f32[6,100,32,128]{3,2,1,0:T(8,128)S(1)} %copy-done, f32[6,100,32,128]{3,2,1,0:T(8,128)S(1)} %copy-done, f32[2,100,32,128]{3,2,1,0:T(8,128)S(1)} %copy-done.2, f32[2,32,128]{2,1,0:T(8,128)S(1)} %get-tuple-element.8.a2d, s32[32,128]{1,0:T(8,128)S(1)} %copy-done.4, ...), custom_call_target="tpu_custom_call" | custom-call | tf_op jit(solution)/shard_map/transport/pallas_call | solution.py:593
Async XLA Ops:
  0.6 65.2 %copy-start = (f32[6,100,32,128]{3,2,1,0:T(8,128)S(1)}, f32[6,100,32,128]{3,2,1,0:T(8,128)}, u32[]{:S(2)}) copy-start(f32[6,100,32,128]{3,2,1,0:T(8,128)} %sa.1) | copy-start | bytes 29491204
  0.6 0.9 %copy-start.3 = (s32[32,128]{1,0:T(8,128)S(1)}, s32[32,128]{1,0:T(8,128)}, u32[]{:S(2)}) copy-start(s32[32,128]{1,0:T(8,128)} %kmt_ref.3) | copy-start | bytes 49156
  1.5 0.9 %copy-start.5 = (f32[3,32,128]{2,1,0:T(8,128)S(1)}, f32[3,32,128]{2,1,0:T(8,128)}, u32[]{:S(2)}) copy-start(f32[3,32,128]{2,1,0:T(8,128)} %baro_ref.1) | copy-start | bytes 147460
  2.5 63.4 %copy-start.4 = (s32[32,128]{1,0:T(8,128)S(1)}, s32[32,128]{1,0:T(8,128)}, u32[]{:S(2)}) copy-start(s32[32,128]{1,0:T(8,128)} %kmt_ref.3) | copy-start | bytes 49156
  64.1 1.7 %copy-start.1 = (f32[2,100,32,128]{3,2,1,0:T(8,128)}, f32[2,100,32,128]{3,2,1,0:T(8,128)S(1)}, u32[]{:S(2)}) copy-start(f32[2,100,32,128]{3,2,1,0:T(8,128)S(1)} %get-tuple-element.7.q) | copy-start | bytes 9830404
  65.8 1.9 %copy-start.2 = (f32[2,100,32,128]{3,2,1,0:T(8,128)S(1)}, f32[2,100,32,128]{3,2,1,0:T(8,128)}, u32[]{:S(2)}) copy-start(f32[2,100,32,128]{3,2,1,0:T(8,128)} %copy-done.1) | copy-start | bytes 9830404

commit v2 on v1

--- a/solution.py
+++ b/solution.py
@@ -10,6 +10,7 @@
 R = 32
 C = 128
 CH = 25
+UNROLL = 5
 NY = 256
 
 DT = 0.1
@@ -42,14 +43,14 @@
 
 
 def kernel_a(
-    layers, kmt_ref, baro_ref,
-    q_out, a2d_out, baro_out, col_out, row_out,
-    uv, s, p, q, cuv, cs,
+    layers, kmt_hbm, baro_hbm,
+    q, s, kmt_ref, a2d_out, baro_out, col_out, row_out,
+    uv, p, baro_ref, cuv, cs,
     m_uv, r_uv, m_p, r_p, m_s, r_s, m_q, r_q,
     d4, corr,
     b1, m1, r1, b2, m2, r2, a0v, r_a0v, r_rows, r_qrows,
     eta, ua, vv, dvv, da, dv, c2, c2a, cfa, cfv, sa, sv,
-    load_sem, out_sem, send_sem, recv_sem,
+    load_sem, send_sem, recv_sem,
 ):
     lon = lax.axis_index("lon")
     lat = lax.axis_index("lat")
@@ -64,6 +65,11 @@
 
     loads = {}
     n_load = 0
+    for name, src, dst in (("kmt", kmt_hbm, kmt_ref), ("baro", baro_hbm, baro_ref)):
+        cp = pltpu.make_async_copy(src, dst, load_sem.at[n_load])
+        cp.start()
+        loads[name] = cp
+        n_load += 1
     for f in range(2):
         cp = pltpu.make_async_copy(layers.at[f], uv.at[f, :, 8:40, :], load_sem.at[n_load])
         cp.start()
@@ -97,6 +103,8 @@
     lane = lanes()
     quad = lane >> 2
     in_quad = lane & 3
+    loads["kmt"].wait()
+    loads["baro"].wait()
     kmt = kmt_ref[...]
     cmask = (kmt > 0).astype(F32)
 
@@ -104,26 +112,43 @@
     b1[2, 40:72, :] = baro_ref[2] * cmask
     b1[3, 40:72, :] = kmt.astype(F32)
 
-    for f in range(2):
-        loads["uv", f].wait()
-
-        def body(j, acc, f=f):
-            xs = []
-            for c in range(4):
-                k = c * CH + j
-                xs.append(jnp.where(k < kmt, uv[f, k, 8:40, :], 0.0))
+    def pack(fields, store=False):
+        def body(j, accs):
             sel = quad == j
             out = []
+            xs = {}
+            for f, (load, masked, _) in enumerate(fields):
+                for c in range(4):
+                    k = c * CH + j
+                    x = load(k)
+                    xs[f, c] = jnp.where(k < kmt, x, 0.0) if masked else x
+            for f in range(len(fields)):
+                for c in range(4):
+                    out.append(jnp.where(sel, roll(xs[f, c], 4 * j + 2), accs[4 * f + c]))
+            if store:
+                for f in range(len(fields)):
+                    for c in range(4):
+                        uv[f, c * CH + j, 8:40, :] = xs[f, c]
+            return tuple(out)
+
+        accs = lax.fori_loop(0, CH, body, (jnp.zeros((R, C), F32),) * (4 * len(fields)), unroll=UNROLL)
+        for f, (_, _, put) in enumerate(fields):
             for c in range(4):
-                out.append(jnp.where(sel, roll(xs[c], 4 * j + 2), acc[c]))
-            for c in range(4):
-                uv[f, c * CH + j, 8:40, :] = xs[c]
-            return tuple(out)
-
-        zero = jnp.zeros((R, C), F32)
-        acc = lax.fori_loop(0, CH, body, (zero,) * 4)
-        for c in range(4):
-            cuv[f, c, 8:40, :] = acc[c]
+                put(c, accs[4 * f + c])
+
+    def put_cuv(f):
+        def put(c, x):
+            cuv[f, c, 8:40, :] = x
+        return put
+
+    def put_cs(f):
+        def put(c, x):
+            cs[f, c] = x
+        return put
+
+    loads["uv", 0].wait()
+    loads["uv", 1].wait()
+    pack([(lambda k, f=f: uv[f, k, 8:40, :], True, put_cuv(f)) for f in range(2)], store=True)
 
     for c in range(4):
         cu, cv = cuv[0, c, 8:40, :], cuv[1, c, 8:40, :]
@@ -147,18 +172,17 @@
         loads["s", c].wait()
 
         def body(j, carry, c=c):
-            csum, total, acc = carry
+            csum, total = carry
             k = c * CH + j
             m = k < kmt
             h = jnp.where(m, s[0, k], 0.0)
             w = ((GRAV * HALINE) * s[2, k] - (GRAV * THERMAL) * s[1, k]) * h
             pk = csum + 0.5 * w
             p[k, 8:40, :] = pk
-            acc = jnp.where(quad == j, roll(pk, 4 * j + 2), acc)
-            return csum + w, total + h, acc
-
-        csum, total, acc = lax.fori_loop(0, CH, body, (csum, total, zero))
-        cs[0, c] = acc
+            return csum + w, total + h
+
+        csum, total = lax.fori_loop(0, CH, body, (csum, total), unroll=UNROLL)
+    pack([(lambda k: p[k, 8:40, :], False, put_cs(0))])
 
     def compact(field, lane_from):
         out = roll(cs[field, 0], -lane_from)
@@ -198,23 +222,15 @@
     send("b1_s", b1.at[:, 40:72, :], b1.at[:, 72:104, :], 0, -1)
     send_sides("b1", m1, r1)
 
+    def pack_scalars(which):
+        pack([(lambda k, f=f: s[f, k], True, put_cs(1 + f)) for f in which])
+        for f in which:
+            m_s[0, f] = compact(1 + f, 1)
+            m_s[1, f] = compact(1 + f, 2)
+
+    pack_scalars((0, 1))
     loads["age"].wait()
-    for f in range(4):
-
-        def body(j, acc, f=f):
-            sel = quad == j
-            out = []
-            for c in range(4):
-                k = c * CH + j
-                x = jnp.where(k < kmt, s[f, k], 0.0)
-                out.append(jnp.where(sel, roll(x, 4 * j + 2), acc[c]))
-            return tuple(out)
-
-        acc = lax.fori_loop(0, CH, body, (zero,) * 4)
-        for c in range(4):
-            cs[1 + f, c] = acc[c]
-        m_s[0, f] = compact(1 + f, 1)
-        m_s[1, f] = compact(1 + f, 2)
+    pack_scalars((2, 3))
     send("s_e", m_s.at[0], r_s.at[0], 1, 0)
     send("s_w", m_s.at[1], r_s.at[1], -1, 0)
     send("s_n", s.at[:, :, 31, :], r_rows.at[0], 0, 1)
@@ -308,14 +324,13 @@
     cor = ROT * (2.0 * (row.astype(F32) + 0.5) / NY - 1.0)
     edge4 = (lane >= 126) | (lane < 2)
 
-    def bilaplace(f, k):
+    def stencil(f, k):
         x = uv[f, k, 8:40, :]
-        a = uv[f, k, 9:41, :] + uv[f, k, 7:39, :]
-        b = uv[f, k, 10:42, :] + uv[f, k, 6:38, :]
-        t = 2.0 * a - 8.0 * x
-        e = roll(roll(x, -1) + t, -1)
-        w = roll(roll(x, 1) + t, 1)
-        return x, e + w + (b - 4.0 * t - 12.0 * x)
+        one = uv[f, k, 9:41, :] + uv[f, k, 7:39, :]
+        two = uv[f, k, 10:42, :] + uv[f, k, 6:38, :]
+        far = -NU * x
+        near = (-2.0 * NU) * one - 8.0 * far
+        return x, far, near, -NU * two - 4.0 * near - 12.0 * far
 
     sums = (zero,) * 4
     for c in range(4):
@@ -324,14 +339,21 @@
             sgu, sgv, squ, sqv, acc = carry
             k = c * CH + j
             m = k < kmt
-            u0, lu = bilaplace(0, k)
-            v0, lv = bilaplace(1, k)
-            pk = p[k, 8:40, :]
+            u0, ufar, unear, gu = stencil(0, k)
+            v0, vfar, vnear, gv = stencil(1, k)
+            hp = 0.5 * p[k, 8:40, :]
             back = lax.rem(126 + C - 4 * j, C)
-            cu = jnp.where(edge4, roll(corr[0, c], back), 0.0)
-            cv = jnp.where(edge4, roll(corr[1, c], back), 0.0)
-            gu = cor * v0 - NU * lu - 0.5 * (roll(pk, -1) - roll(pk, 1)) + cu
-            gv = cv - cor * u0 - NU * lv - 0.5 * (p[k, 9:41, :] - p[k, 7:39, :])
+            cu = roll(corr[0, c], back)
+            cv = roll(corr[1, c], back)
+            ue = roll(unear - hp, -1)
+            uw = roll(unear + hp, 1)
+            uee, uww = roll(ufar, -2), roll(ufar, 2)
+            ve, vw = roll(vnear, -1), roll(vnear, 1)
+            vee, vww = roll(vfar, -2), roll(vfar, 2)
+            gu = gu + cor * v0
+            gv = gv - cor * u0 - 0.5 * (p[k, 9:41, :] - p[k, 7:39, :])
+            gu = gu + jnp.where(edge4, cu, 0.0) + ((ue + uw) + (uee + uww))
+            gv = gv + jnp.where(edge4, cv, 0.0) + ((ve + vw) + (vee + vww))
             gu = jnp.where(m, gu, 0.0)
             gv = jnp.where(m, gv, 0.0)
             qu = u0 + DT * gu
@@ -342,15 +364,9 @@
             acc = jnp.where(quad == j, roll(qu, 4 * j + 2), acc)
             return sgu + gu * h, sgv + gv * h, squ + qu * h, sqv + qv * h, acc
 
-        *sums, acc = lax.fori_loop(0, CH, body, (*sums, zero))
+        *sums, acc = lax.fori_loop(0, CH, body, (*sums, zero), unroll=UNROLL)
         cs[0, c] = acc
     sgu, sgv, squ, sqv = sums
-
-    out_copies = []
-    for f in range(2):
-        cp = pltpu.make_async_copy(q.at[f], q_out.at[f], out_sem.at[f])
-        cp.start()
-        out_copies.append(cp)
 
     bound = jnp.maximum(total, 1.0)
     fu, fv = sgu / bound, sgv / bound
@@ -470,8 +486,6 @@
 
     for cp in copies.values():
         cp.wait_send()
-    for cp in out_copies:
-        cp.wait()
 
 
 N_COPIES = 2 + 6 + 2 + 4 + 2 + 6 + 4 + 2 + 6 + 2 + 4
@@ -480,41 +494,29 @@
 def call_a(layers, kmt, baro):
     v = lambda *shape: pltpu.VMEM(shape, F32)
     surface = [v(2, 112, C) for _ in range(10)]
+    vmem = pl.BlockSpec(memory_space=pltpu.VMEM)
+    shape = lambda *dims: jax.ShapeDtypeStruct(dims, F32)
     return pl.pallas_call(
         kernel_a,
         out_shape=(
-            jax.ShapeDtypeStruct((2, K, R, C), F32),
-            jax.ShapeDtypeStruct((2, R, C), F32),
-            jax.ShapeDtypeStruct((3, R, C), F32),
-            jax.ShapeDtypeStruct((4, 2, R, C), F32),
-            jax.ShapeDtypeStruct((8, K, C), F32),
+            shape(2, K, R, C), shape(4, K, R, C), jax.ShapeDtypeStruct((R, C), jnp.int32),
+            shape(2, R, C), shape(3, R, C), shape(4, 2, R, C), shape(8, K, C),
         ),
-        in_specs=[
-            pl.BlockSpec(memory_space=pl.ANY),
-            pl.BlockSpec(memory_space=pltpu.VMEM),
-            pl.BlockSpec(memory_space=pltpu.VMEM),
-        ],
-        out_specs=(
-            pl.BlockSpec(memory_space=pl.ANY),
-            pl.BlockSpec(memory_space=pltpu.VMEM),
-            pl.BlockSpec(memory_space=pltpu.VMEM),
-            pl.BlockSpec(memory_space=pltpu.VMEM),
-            pl.BlockSpec(memory_space=pltpu.VMEM),
-        ),
+        in_specs=[pl.BlockSpec(memory_space=pltpu.HBM)] * 3,
+        out_specs=(vmem,) * 7,
         scratch_shapes=[
-            v(2, K, 48, C), v(4, K, R, C), v(K, 48, C), v(2, K, R, C), v(2, 4, 48, C), v(5, 4, R, C),
+            v(2, K, 48, C), v(K, 48, C), v(3, R, C), v(2, 4, 48, C), v(5, 4, R, C),
             v(2, 4, R, C), v(2, 4, 48, C), v(2, R, C), v(2, R, C), v(2, 4, R, C), v(2, 4, R, C), v(2, R, C), v(2, R, C),
             v(2, 4, 48, C), v(2, 4, R, C),
             v(4, 112, C), v(2, R, C), v(2, 96, C), v(3, 112, C), v(2, R, C), v(2, 96, C),
             v(R, C), v(2, 8, C), v(2, 4, K, C), v(2, K, C),
             *surface, v(2, R, C), v(48, C),
-            pltpu.SemaphoreType.DMA((7,)),
-            pltpu.SemaphoreType.DMA((2,)),
+            pltpu.SemaphoreType.DMA((9,)),
             pltpu.SemaphoreType.DMA((N_COPIES,)),
             pltpu.SemaphoreType.DMA((N_COPIES,)),
         ],
         compiler_params=pltpu.CompilerParams(
-            collective_id=0, has_side_effects=True, vmem_limit_bytes=50 * 2**20),
+            collective_id=0, has_side_effects=True, vmem_limit_bytes=42 * 2**20),
         name="tendencies_and_surface",
     )(layers, kmt, baro)
 
@@ -522,17 +524,15 @@
 LB = 10
 
 
-def kernel_b(ht, sa, q, a2d, kmt_ref, col, rows, baro, out, baro_out):
-    step = pl.program_id(0)
+def kernel_b(q, s, kmt_ref, a2d, baro, col, rows, out_hbm, baro_hbm, out, out_sem):
     lane = lanes()
     sub = sublanes((8, C))
     kmt = kmt_ref[...]
     au, av = a2d[0], a2d[1]
     kd = DT * KAPPA
 
-    @pl.when(step == 0)
-    def _():
-        baro_out[...] = baro[...]
+    copies = [pltpu.make_async_copy(baro, baro_hbm, out_sem.at[K // LB])]
+    copies[0].start()
 
     def tiles(x):
         return [x[8 * i:8 * i + 8] for i in range(4)]
@@ -545,18 +545,17 @@
         r = [jnp.broadcast_to(halo, (8, C))] + [pltpu.roll(t, 1, axis=0) for t in tiles(x)]
         return jnp.concatenate([jnp.where(sub == 0, r[i], r[i + 1]) for i in range(4)], axis=0)
 
-    def body(l, carry):
-        k = step * LB + l
+    def body(k, carry):
         c = k // CH
         j = k - c * CH
         tile = k // (2 * CH)
         back = 127 - 4 * j - 2 * (c - 2 * tile)
         m = k < kmt
-        h = ht[0, l]
-        un = jnp.where(m, q[0, l] + au, 0.0)
-        vn = jnp.where(m, q[1, l] + av, 0.0)
-        out[0, l] = un
-        out[1, l] = vn
+        h = s[0, k]
+        un = jnp.where(m, q[0, k] + au, 0.0)
+        vn = jnp.where(m, q[1, k] + av, 0.0)
+        out[0, k] = un
+        out[1, k] = vn
         h5 = (0.5 * DT) * h
         fu, fv = h5 * un, h5 * vn
 
@@ -573,48 +572,49 @@
         e = jnp.where(lane == 127, hal, roll(fu, -1))
         w = jnp.where(lane == 0, hal, roll(fu, 1))
         hn = h - ((e - w) + (from_north(fv, row_n(0)) - from_south(fv, row_s(0))))
-        out[2, l] = jnp.where(m, hn, 0.0)
+        out[2, k] = jnp.where(m, hn, 0.0)
         ke, kw, kn, ks = kd - fu, kd + fu, kd - fv, kd + fv
         mid = h - 4.0 * kd
-        for n, (ref, at) in enumerate(((ht, 1), (sa, 0), (sa, 1)), start=1):
-            x = jnp.where(m, ref[at, l], 0.0)
+        for n in range(1, 4):
+            x = jnp.where(m, s[n, k], 0.0)
             hal = halo(n)
             e = jnp.where(lane == 127, hal, roll(x * ke, -1))
             w = jnp.where(lane == 0, hal, roll(x * kw, 1))
             r = from_north(x * kn, row_n(n)) + from_south(x * ks, row_s(n))
-            out[2 + n, l] = jnp.where(m, (e + w) + (r + x * mid), 0.0)
+            out[2 + n, k] = jnp.where(m, (e + w) + (r + x * mid), 0.0)
         return carry
 
-    lax.fori_loop(0, LB, body, 0)
-
-
-def call_b(layers, q, a2d, kmt, col, rows, baro):
-    whole = lambda *shape: pl.BlockSpec(shape, lambda i: (0,) * len(shape))
+    for i in range(K // LB):
+        at = slice(i * LB, (i + 1) * LB)
+        lax.fori_loop(i * LB, (i + 1) * LB, body, 0, unroll=UNROLL)
+        cp = pltpu.make_async_copy(out.at[:, at], out_hbm.at[:, at], out_sem.at[i])
+        cp.start()
+        copies.append(cp)
+    for cp in copies:
+        cp.wait()
+
+
+def call_b(*operands):
+    hbm = pl.BlockSpec(memory_space=pltpu.HBM)
     return pl.pallas_call(
         kernel_b,
-        grid=(K // LB,),
         out_shape=(
             jax.ShapeDtypeStruct((6, K, R, C), F32),
             jax.ShapeDtypeStruct((3, R, C), F32),
         ),
-        in_specs=[
-            pl.BlockSpec((2, LB, R, C), lambda i: (1, i, 0, 0)),
-            pl.BlockSpec((2, LB, R, C), lambda i: (2, i, 0, 0)),
-            pl.BlockSpec((2, LB, R, C), lambda i: (0, i, 0, 0)),
-            whole(2, R, C), whole(R, C), whole(4, 2, R, C), whole(8, K, C), whole(3, R, C),
+        in_specs=[pl.BlockSpec(memory_space=pltpu.VMEM)] * len(operands),
+        out_specs=(hbm, hbm),
+        scratch_shapes=[
+            pltpu.VMEM((6, K, R, C), F32),
+            pltpu.SemaphoreType.DMA((K // LB + 1,)),
         ],
-        out_specs=(
-            pl.BlockSpec((6, LB, R, C), lambda i: (0, i, 0, 0)),
-            whole(3, R, C),
-        ),
-        compiler_params=pltpu.CompilerParams(vmem_limit_bytes=40 * 2**20),
+        compiler_params=pltpu.CompilerParams(vmem_limit_bytes=24 * 2**20),
         name="transport",
-    )(layers, layers, q, a2d, kmt, col, rows, baro)
+    )(*operands)
 
 
 def per_device(layers, kmt, barotropic):
-    q, a2d, baro, col, rows = call_a(layers, kmt, barotropic)
-    return call_b(layers, q, a2d, kmt, col, rows, baro)
+    return call_b(*call_a(layers, kmt, barotropic))
 
 
 def solution(mesh):

time: 83.2 us -> 47.1 us (0.57)
  Pallas kernels: 76.3 us -> 44.7 us
  local copies, waits for them, and re-layouts: 5.44 us -> 1.51 us
    pallas_call x2, Pallas kernels: 76.3 us -> 44.7 us  [the longest x1 36.8 us: call_a(): pl.pallas_call(kernel_a, out_shape=(shape(2, K, R, C), shape(4, K, R, C),...]
    unnamed x12 -> x4, local copies, waits for them, and re-layouts: 5.44 us -> 1.51 us
where the time goes in v2:
time: 47.1 us; the launch traced here: 46.8 us
  Pallas kernels  44.7 us (95%)
  local copies, waits for them, and re-layouts  1.51 us (3%)
  between operations  0.65 us (1%)
    pallas_call x1, Pallas kernels, call_a(): pl.pallas_call(kernel_a, out_shape=(shape(2, K, R, C), shape(4, K, R, C),...  36.8 us
    pallas_call x1, Pallas kernels, call_b(): pl.pallas_call(kernel_b, out_shape=(jax.ShapeDtypeStruct((6, K, R, C), F3...  7.87 us
    unnamed x4, local copies, waits for them, and re-layouts  1.51 us

profile of v2, /device:TPU:0, one launch (start us, length us, event | category | flops | bytes accessed | tf_op | source)
XLA Modules:
  0.0 46.8 jit_solution(14967298254027266707)
XLA Ops:
  0.6 0.0 copy-start
  0.6 0.8 %copy-done = f32[3,32,128]{2,1,0:T(8,128)S(1)} copy-done((f32[3,32,128]{2,1,0:T(8,128)S(1)}, f32[3,32,128]{2,1,0:T(8,128)}, u32[]{:S(2)}) %copy-start) | copy-done | bytes 49176
  1.4 0.0 copy-start.1
  1.4 0.7 %copy-done.1 = s32[32,128]{1,0:T(8,128)S(1)} copy-done((s32[32,128]{1,0:T(8,128)S(1)}, s32[32,128]{1,0:T(8,128)}, u32[]{:S(2)}) %copy-start.1) | copy-done | bytes 16408
  2.1 36.8 %tendencies_and_surface.1 = (f32[2,100,32,128]{3,2,1,0:T(8,128)S(1)}, f32[4,100,32,128]{3,2,1,0:T(8,128)S(1)}, s32[32,128]{1,0:T(8,128)S(1)}, f32[2,32,128]{2,1,...) custom-call(f32[6,100,32,128]{3,2,1,0:T(8,128)} %layers.1, ...), custom_call_target="tpu_custom_call" | custom-call | tf_op jit(solution)/shard_map/tendencies_and_surface/pallas_call | solution.py:499
  39.0 7.9 %transport.1 = (f32[6,100,32,128]{3,2,1,0:T(8,128)}, f32[3,32,128]{2,1,0:T(8,128)}) custom-call(f32[2,100,32,128]{3,2,1,0:T(8,128)S(1)} %get-tuple-element.9.q, f32[4,100,32,128]{3,2,1,0:T(8,128)S(1)} %get-tuple-element.10.s, s32[32,128]{1,0:T(8,128)S(1)} %get-tuple-element.11.kmt_ref, f32[2,32,128]{2,1,0:T(8,128)S(1)} %get-tuple-element.12.a2d, ...), custom_call_target="tpu_custom_call" | custom-call | tf_op jit(solution)/shard_map/transport/pallas_call | solution.py:599
Async XLA Ops:
  0.6 0.8 %copy-start = (f32[3,32,128]{2,1,0:T(8,128)S(1)}, f32[3,32,128]{2,1,0:T(8,128)}, u32[]{:S(2)}) copy-start(f32[3,32,128]{2,1,0:T(8,128)} %baro_hbm.1) | copy-start | bytes 147460
  1.4 0.7 %copy-start.1 = (s32[32,128]{1,0:T(8,128)S(1)}, s32[32,128]{1,0:T(8,128)}, u32[]{:S(2)}) copy-start(s32[32,128]{1,0:T(8,128)} %kmt_hbm.1) | copy-start | bytes 49156

commit v3 on v2

--- a/solution.py
+++ b/solution.py
@@ -22,7 +22,10 @@
 HALINE = 0.8
 ROT = 0.5
 
+PSCALE = 1.0 / (4.0 * NU)
+
 F32 = jnp.float32
+BF16 = jnp.bfloat16
 MESH = pl.DeviceIdType.MESH
 
 
@@ -32,6 +35,14 @@
 
 def sublanes(shape):
     return lax.broadcasted_iota(jnp.int32, shape, 0)
+
+
+def split(x, parts):
+    out = []
+    for _ in range(parts):
+        out.append(x.astype(BF16))
+        x = x - out[-1].astype(F32)
+    return jnp.concatenate(out, axis=1)
 
 
 def roll(x, s):
@@ -45,9 +56,9 @@
 def kernel_a(
     layers, kmt_hbm, baro_hbm,
     q, s, kmt_ref, a2d_out, baro_out, col_out, row_out,
-    uv, p, baro_ref, cuv, cs,
+    uv, p, baro_ref, cuv, cs, q_edge,
     m_uv, r_uv, m_p, r_p, m_s, r_s, m_q, r_q,
-    d4, corr,
+    d4, corr, shift,
     b1, m1, r1, b2, m2, r2, a0v, r_a0v, r_rows, r_qrows,
     eta, ua, vv, dvv, da, dv, c2, c2a, cfa, cfv, sa, sv,
     load_sem, send_sem, recv_sem,
@@ -70,17 +81,18 @@
         cp.start()
         loads[name] = cp
         n_load += 1
-    for f in range(2):
-        cp = pltpu.make_async_copy(layers.at[f], uv.at[f, :, 8:40, :], load_sem.at[n_load])
+    half = [slice(0, K // 2), slice(K // 2, K)]
+    for i in range(2):
+        cp = pltpu.make_async_copy(layers.at[0:2, half[i]], uv.at[0:2, half[i], 8:40, :], load_sem.at[n_load])
         cp.start()
-        loads["uv", f] = cp
+        loads["uv", i] = cp
         n_load += 1
-    for c in range(4):
-        cp = pltpu.make_async_copy(
-            layers.at[2:5, c * CH:(c + 1) * CH], s.at[0:3, c * CH:(c + 1) * CH], load_sem.at[n_load])
-        cp.start()
-        loads["s", c] = cp
-        n_load += 1
+        for c in (2 * i, 2 * i + 1):
+            cp = pltpu.make_async_copy(
+                layers.at[2:5, c * CH:(c + 1) * CH], s.at[0:3, c * CH:(c + 1) * CH], load_sem.at[n_load])
+            cp.start()
+            loads["s", c] = cp
+            n_load += 1
     cp = pltpu.make_async_copy(layers.at[5], s.at[3], load_sem.at[n_load])
     cp.start()
     loads["age"] = cp
@@ -108,33 +120,30 @@
     kmt = kmt_ref[...]
     cmask = (kmt > 0).astype(F32)
 
+    for c in range(4):
+        q_edge[c] = jnp.zeros((R, C), F32)
+
     b1[1, 40:72, :] = baro_ref[1] * cmask
     b1[2, 40:72, :] = baro_ref[2] * cmask
     b1[3, 40:72, :] = kmt.astype(F32)
 
-    def pack(fields, store=False):
+    def pack(fields):
         def body(j, accs):
             sel = quad == j
-            out = []
-            xs = {}
-            for f, (load, masked, _) in enumerate(fields):
-                for c in range(4):
-                    k = c * CH + j
-                    x = load(k)
-                    xs[f, c] = jnp.where(k < kmt, x, 0.0) if masked else x
-            for f in range(len(fields)):
-                for c in range(4):
-                    out.append(jnp.where(sel, roll(xs[f, c], 4 * j + 2), accs[4 * f + c]))
-            if store:
-                for f in range(len(fields)):
-                    for c in range(4):
-                        uv[f, c * CH + j, 8:40, :] = xs[f, c]
-            return tuple(out)
-
-        accs = lax.fori_loop(0, CH, body, (jnp.zeros((R, C), F32),) * (4 * len(fields)), unroll=UNROLL)
-        for f, (_, _, put) in enumerate(fields):
-            for c in range(4):
-                put(c, accs[4 * f + c])
+            xs = []
+            for load, masked, _, _, c in fields:
+                k = c * CH + j
+                x = load(k)
+                xs.append(jnp.where(k < kmt, x, 0.0) if masked else x)
+            out = tuple(jnp.where(sel, roll(x, 4 * j + 2), acc) for x, acc in zip(xs, accs))
+            for x, (_, _, store, _, c) in zip(xs, fields):
+                if store is not None:
+                    uv[store, c * CH + j, 8:40, :] = x
+            return out
+
+        accs = lax.fori_loop(0, CH, body, (jnp.zeros((R, C), F32),) * len(fields), unroll=UNROLL)
+        for (_, _, _, put, c), acc in zip(fields, accs):
+            put(c, acc)
 
     def put_cuv(f):
         def put(c, x):
@@ -146,25 +155,53 @@
             cs[f, c] = x
         return put
 
+    def velocities(i):
+        return [(lambda k, f=f: uv[f, k, 8:40, :], True, f, put_cuv(f), c) for f in range(2) for c in (2 * i, 2 * i + 1)]
+
+    def pressures(i):
+        return [(lambda k: p[k, 8:40, :], False, None, put_cs(0), c) for c in (2 * i, 2 * i + 1)]
+
+    def scalars(f):
+        return [(lambda k: s[f, k], True, None, put_cs(1 + f), c) for c in range(4)]
+
+    def compact(field, lane_from, chunks=(0, 1, 2, 3)):
+        out = roll(cs[field, chunks[0]], chunks[0] - lane_from)
+        for c in chunks[1:]:
+            out = jnp.where(in_quad == c, roll(cs[field, c], c - lane_from), out)
+        return out
+
+    def send_velocities(i):
+        both = slice(2 * i, 2 * i + 2)
+        for c in (2 * i, 2 * i + 1):
+            cu, cv = cuv[0, c, 8:40, :], cuv[1, c, 8:40, :]
+            m_uv[0, c] = jnp.where(in_quad < 2, cu, roll(cv, 2))
+            m_uv[1, c] = jnp.where(in_quad < 2, roll(cu, -2), cv)
+        for d, dx in ((0, 1), (1, -1)):
+            send(("uv", dx, 1, i), m_uv.at[d, both, 31:32, :], r_uv.at[d, both, 7:8, :], dx, 1)
+            send(("uv", dx, -1, i), m_uv.at[d, both, 0:1, :], r_uv.at[d, both, 40:41, :], dx, -1)
+            send(("uv", dx, 0, i), m_uv.at[d, both], r_uv.at[d, both, 8:40, :], dx, 0)
+        send(("cuv_n", i), cuv.at[:, both, 39:40, :], cuv.at[:, both, 7:8, :], 0, 1)
+        send(("cuv_s", i), cuv.at[:, both, 8:9, :], cuv.at[:, both, 40:41, :], 0, -1)
+
+    def send_pressures(i):
+        m_p[i, 0] = compact(0, 1, (2 * i, 2 * i + 1))
+        m_p[i, 1] = compact(0, 2, (2 * i, 2 * i + 1))
+        send(("p_e", i), m_p.at[i, 0], r_p.at[i, 0], 1, 0)
+        send(("p_w", i), m_p.at[i, 1], r_p.at[i, 1], -1, 0)
+        send(("p_n", i), p.at[half[i], 39, :], p.at[half[i], 7, :], 0, 1)
+        send(("p_s", i), p.at[half[i], 8, :], p.at[half[i], 40, :], 0, -1)
+
     loads["uv", 0].wait()
-    loads["uv", 1].wait()
-    pack([(lambda k, f=f: uv[f, k, 8:40, :], True, put_cuv(f)) for f in range(2)], store=True)
-
-    for c in range(4):
-        cu, cv = cuv[0, c, 8:40, :], cuv[1, c, 8:40, :]
-        m_uv[0, c] = jnp.where(in_quad < 2, cu, roll(cv, 2))
-        m_uv[1, c] = jnp.where(in_quad < 2, roll(cu, -2), cv)
+    pack(velocities(0))
 
     pl.semaphore_wait(barrier, 8)
-
-    send("uv_n", uv.at[:, :, 38:40, :], uv.at[:, :, 6:8, :], 0, 1)
-    send("uv_s", uv.at[:, :, 8:10, :], uv.at[:, :, 40:42, :], 0, -1)
-    for d, dx in ((0, 1), (1, -1)):
-        send(("uv", dx, 0), m_uv.at[d], r_uv.at[d, :, 8:40, :], dx, 0)
-        send(("uv", dx, 1), m_uv.at[d, :, 24:32, :], r_uv.at[d, :, 0:8, :], dx, 1)
-        send(("uv", dx, -1), m_uv.at[d, :, 0:8, :], r_uv.at[d, :, 40:48, :], dx, -1)
-    send("cuv_n", cuv.at[:, :, 32:40, :], cuv.at[:, :, 0:8, :], 0, 1)
-    send("cuv_s", cuv.at[:, :, 8:16, :], cuv.at[:, :, 40:48, :], 0, -1)
+    for i in range(2):
+        send(("uv_n", i), layers.at[0:2, half[i], 30:32, :], uv.at[:, half[i], 6:8, :], 0, 1)
+        send(("uv_s", i), layers.at[0:2, half[i], 0:2, :], uv.at[:, half[i], 40:42, :], 0, -1)
+        if i == 0:
+            send("b1_n", b1.at[1:4, 40:72, :], b1.at[1:4, 8:40, :], 0, 1)
+            send("b1_s", b1.at[1:4, 40:72, :], b1.at[1:4, 72:104, :], 0, -1)
+    send_velocities(0)
 
     zero = jnp.zeros((R, C), F32)
     csum, total = zero, zero
@@ -176,22 +213,18 @@
             k = c * CH + j
             m = k < kmt
             h = jnp.where(m, s[0, k], 0.0)
-            w = ((GRAV * HALINE) * s[2, k] - (GRAV * THERMAL) * s[1, k]) * h
+            w = ((PSCALE * GRAV * HALINE) * s[2, k] - (PSCALE * GRAV * THERMAL) * s[1, k]) * h
             pk = csum + 0.5 * w
             p[k, 8:40, :] = pk
             return csum + w, total + h
 
         csum, total = lax.fori_loop(0, CH, body, (csum, total), unroll=UNROLL)
-    pack([(lambda k: p[k, 8:40, :], False, put_cs(0))])
-
-    def compact(field, lane_from):
-        out = roll(cs[field, 0], -lane_from)
-        for c in range(1, 4):
-            out = jnp.where(in_quad == c, roll(cs[field, c], c - lane_from), out)
-        return out
-
-    m_p[0] = compact(0, 1)
-    m_p[1] = compact(0, 2)
+        if c == 1:
+            loads["uv", 1].wait()
+            pack(pressures(0) + velocities(1))
+            send_pressures(0)
+            send_velocities(1)
+
     b1[0, 40:72, :] = total * (1.0 / K)
 
     def side(fields, eastward):
@@ -210,41 +243,25 @@
 
     def send_sides(tag, m, r):
         for d, dx in ((0, 1), (1, -1)):
-            send((tag, dx, 0), m.at[d], r.at[d, 32:64, :], dx, 0)
             send((tag, dx, 1), m.at[d], r.at[d, 0:32, :], dx, 1)
             send((tag, dx, -1), m.at[d], r.at[d, 64:96, :], dx, -1)
-
-    send("p_e", m_p.at[0], r_p.at[0], 1, 0)
-    send("p_w", m_p.at[1], r_p.at[1], -1, 0)
-    send("p_n", p.at[:, 39, :], p.at[:, 7, :], 0, 1)
-    send("p_s", p.at[:, 8, :], p.at[:, 40, :], 0, -1)
-    send("b1_n", b1.at[:, 40:72, :], b1.at[:, 8:40, :], 0, 1)
-    send("b1_s", b1.at[:, 40:72, :], b1.at[:, 72:104, :], 0, -1)
+            send((tag, dx, 0), m.at[d], r.at[d, 32:64, :], dx, 0)
+
+    send("d_n", b1.at[0, 40:72, :], b1.at[0, 8:40, :], 0, 1)
+    send("d_s", b1.at[0, 40:72, :], b1.at[0, 72:104, :], 0, -1)
     send_sides("b1", m1, r1)
 
-    def pack_scalars(which):
-        pack([(lambda k, f=f: s[f, k], True, put_cs(1 + f)) for f in which])
+    def send_scalars(which):
         for f in which:
             m_s[0, f] = compact(1 + f, 1)
             m_s[1, f] = compact(1 + f, 2)
 
-    pack_scalars((0, 1))
+    pack(pressures(1) + scalars(0))
+    send_pressures(1)
+    pack(scalars(1))
     loads["age"].wait()
-    pack_scalars((2, 3))
-    send("s_e", m_s.at[0], r_s.at[0], 1, 0)
-    send("s_w", m_s.at[1], r_s.at[1], -1, 0)
     send("s_n", s.at[:, :, 31, :], r_rows.at[0], 0, 1)
     send("s_s", s.at[:, :, 0, :], r_rows.at[1], 0, -1)
-
-    for name in ("b1_n", "b1_s"):
-        copies[name].wait_recv()
-    for dx in (1, -1):
-        for dy in (0, 1, -1):
-            copies["b1", dx, dy].wait_recv()
-    for ref in (eta, dvv):
-        for t in range(2):
-            ref[t, 0:8, :] = jnp.zeros((8, C), F32)
-            ref[t, 104:112, :] = jnp.zeros((8, C), F32)
 
     def tiles_of(n, centre, r, at):
         lo, hi = at
@@ -256,23 +273,6 @@
     def shift_west(t0, t1):
         a, b = roll(t0, 1), roll(t1, 1)
         return jnp.where(lane < 1, b, a), jnp.where(lane < 1, a, b)
-
-    for blk in range(3):
-        at = (32 * blk, 32 * blk + 32)
-        here = slice(8 + 32 * blk, 40 + 32 * blk)
-        dd = tiles_of(0, b1, r1, at)
-        uu = tiles_of(1, b1, r1, at)
-        ww = tiles_of(2, b1, r1, at)
-        dda = shift_west(*dd)
-        uua = shift_west(*uu)
-        for t in range(2):
-            da[t, here, :] = dda[t]
-            ua[t, here, :] = uua[t]
-            dv[t, here, :] = dd[t]
-            vv[t, here, :] = ww[t]
-            dvv[t, here, :] = dd[t] * ww[t]
-            c2[t, here, :] = jnp.where(dd[t] > 0.0, 0.5 * TAU, 0.0)
-            c2a[t, here, :] = jnp.where(dda[t] > 0.0, 0.5 * TAU, 0.0)
 
     def next_height(lo, both):
         n = 2 if both else 1
@@ -286,90 +286,146 @@
             out.append(c2[t, at, :] * diff)
         return out
 
-    for i in range(4):
-        drop = next_height(40 + 8 * i, False)[0]
-        b2[2, 40 + 8 * i:48 + 8 * i, :] = (
-            baro_ref[0, 8 * i:8 * i + 8, :] * cmask[8 * i:8 * i + 8] - drop)
-
-    for name in ("cuv_n", "cuv_s"):
+    def prepare_surface():
+        for name in ("d_n", "d_s"):
+            copies[name].wait_recv()
+        for dx in (1, -1):
+            for dy in (0, 1, -1):
+                copies["b1", dx, dy].wait_recv()
+        for ref in (eta, dvv):
+            for t in range(2):
+                ref[t, 0:8, :] = jnp.zeros((8, C), F32)
+                ref[t, 104:112, :] = jnp.zeros((8, C), F32)
+        for blk in range(3):
+            at = (32 * blk, 32 * blk + 32)
+            here = slice(8 + 32 * blk, 40 + 32 * blk)
+            dd = tiles_of(0, b1, r1, at)
+            uu = tiles_of(1, b1, r1, at)
+            ww = tiles_of(2, b1, r1, at)
+            dda = shift_west(*dd)
+            uua = shift_west(*uu)
+            for t in range(2):
+                da[t, here, :] = dda[t]
+                ua[t, here, :] = uua[t]
+                dv[t, here, :] = dd[t]
+                vv[t, here, :] = ww[t]
+                dvv[t, here, :] = dd[t] * ww[t]
+                c2[t, here, :] = jnp.where(dd[t] > 0.0, 0.5 * TAU, 0.0)
+                c2a[t, here, :] = jnp.where(dda[t] > 0.0, 0.5 * TAU, 0.0)
+
+        for i in range(4):
+            drop = next_height(40 + 8 * i, False)[0]
+            b2[2, 40 + 8 * i:48 + 8 * i, :] = (
+                baro_ref[0, 8 * i:8 * i + 8, :] * cmask[8 * i:8 * i + 8] - drop)
+
+    def correct(i):
+        for name in ("cuv_n", "cuv_s", "p_e", "p_w", "uv_n", "uv_s", "p_n", "p_s"):
+            copies[name, i].wait_recv()
+        for dx in (1, -1):
+            for dy in (0, 1, -1):
+                copies["uv", dx, dy, i].wait_recv()
+        p_w, p_e = r_p[i, 0], r_p[i, 1]
+        for c in (2 * i, 2 * i + 1):
+            w, e = r_uv[0, c], r_uv[1, c]
+            d4[0, c] = jnp.where(in_quad < 2, w, roll(e, 2)) - cuv[0, c]
+            d4[1, c] = jnp.where(in_quad < 2, roll(w, -2), e) - cuv[1, c]
+        for c in (2 * i, 2 * i + 1):
+            for f in range(2):
+                x = d4[f, c, 8:40, :]
+                g = 2.0 * (d4[f, c, 9:41, :] + d4[f, c, 7:39, :]) - 8.0 * x
+                out = jnp.where(in_quad < 2, roll(x, -2), roll(x, 2))
+                out = out + jnp.where(in_quad == 1, roll(g, -1), jnp.where(in_quad == 2, roll(g, 1), 0.0))
+                out = 0.5 * out
+                if f == 0:
+                    own = cs[0, c]
+                    at_127 = roll(p_e, 1 - c) - roll(own, -1)
+                    at_0 = roll(own, 1) - roll(p_w, 2 - c)
+                    out = out + jnp.where(in_quad == 1, at_127, jnp.where(in_quad == 2, at_0, 0.0))
+                corr[f, c] = split(out, 3)
+
+    for name in ("b1_n", "b1_s"):
         copies[name].wait_recv()
-    for dx in (1, -1):
-        for dy in (0, 1, -1):
-            copies["uv", dx, dy].wait_recv()
+
+    row = sublanes((R, C)) + lat * R
+    cor = DT * ROT * (2.0 * (row.astype(F32) + 0.5) / NY - 1.0)
+
+    rim = {at: b1[3, at + 32:at + 40, :] for at in (6, 7, 33, 34)}
+
+    def shifted(f, k, by, seen):
+        lo = 8 + by
+        x = uv[f, k, lo:lo + R, :]
+        at = lo if by < 0 else lo + 24
+        if by < 0:
+            return jnp.concatenate([jnp.where(seen[at], x[0:8], 0.0), x[8:]], axis=0)
+        return jnp.concatenate([x[:24], jnp.where(seen[at], x[24:], 0.0)], axis=0)
+
+    def stencil(f, k, seen):
+        x = uv[f, k, 8:40, :]
+        one = shifted(f, k, 1, seen) + shifted(f, k, -1, seen)
+        two = shifted(f, k, 2, seen) + shifted(f, k, -2, seen)
+        return x, one - 4.0 * x, 0.5 * two + (10.0 * x - 4.0 * one)
+
+    i = lax.broadcasted_iota(jnp.int32, (5 * C, C), 0)
+    to = lax.broadcasted_iota(jnp.int32, (5 * C, C), 1)
+    apart = (to - i) & (C - 1)
+    far = jnp.where((apart == 2) | (apart == C - 2), 0.5, 0.0)
+    edge = jnp.where(to == ((126 + (i & 3)) & (C - 1)), 1.0, 0.0)
+    shift[...] = jnp.where(i < 2 * C, far, edge).astype(BF16)
+    quad3 = lax.broadcasted_iota(jnp.int32, (1, 3 * C), 1) % C >> 2
+
+    def level(k, j, extra, sums, acc):
+        sgu, sgv, squ, sqv = sums
+        m = k < kmt
+        kf = k.astype(F32)
+        seen = {at: kf < x for at, x in rim.items()}
+        u0, unear, gu = stencil(0, k, seen)
+        v0, vnear, gv = stencil(1, k, seen)
+        pk = p[k, 8:40, :]
+        ue = roll(unear + pk, -1)
+        uw = roll(unear - pk, 1)
+        ve, vw = roll(vnear, -1), roll(vnear, 1)
+        gv = gv + (p[k, 9:41, :] - p[k, 7:39, :])
+        gu = (gu + extra[0]) + (ue + uw)
+        gv = (gv + extra[1]) + (ve + vw)
+        gu = jnp.where(m, cor * v0 - (2.0 * DT * NU) * gu, 0.0)
+        gv = jnp.where(m, -cor * u0 - (2.0 * DT * NU) * gv, 0.0)
+        qu = u0 + gu
+        qv = v0 + gv
+        q[0, k] = qu
+        q[1, k] = qv
+        h = s[0, k]
+        acc = jnp.where(quad == j, roll(qu, 4 * j + 2), acc)
+        return (sgu + gu * h, sgv + gv * h, squ + qu * h, sqv + qv * h), acc
+
+    sums = (zero,) * 4
+    for i in range(2):
+        correct(i)
+
+        def body(n, sums):
+            c = n // 5
+            acc = zero
+            j0 = 5 * (n - 5 * c)
+            left = []
+            for l in range(5):
+                on = (quad3 == j0 + l).astype(F32).astype(BF16)
+                for f in range(2):
+                    left.append(jnp.concatenate([split(uv[f, 5 * n + l, 8:40, :], 2), corr[f, c] * on], axis=1))
+            moved = jnp.dot(jnp.concatenate(left, axis=0), shift[...], preferred_element_type=F32)
+            for l in range(5):
+                extra = [moved[R * (2 * l + f):R * (2 * l + f + 1)] for f in range(2)]
+                sums, acc = level(5 * n + l, j0 + l, extra, sums, acc)
+            q_edge[c] = q_edge[c] + acc
+            return sums
+
+        sums = lax.fori_loop(10 * i, 10 * i + 10, body, sums)
+        if i == 0:
+            prepare_surface()
     for c in range(4):
-        w, e = r_uv[0, c], r_uv[1, c]
-        d4[0, c] = jnp.where(in_quad < 2, w, roll(e, 2)) - cuv[0, c]
-        d4[1, c] = jnp.where(in_quad < 2, roll(w, -2), e) - cuv[1, c]
-    copies["p_e"].wait_recv()
-    copies["p_w"].wait_recv()
-    p_w, p_e = r_p[0], r_p[1]
-    for c in range(4):
-        for f in range(2):
-            x = d4[f, c, 8:40, :]
-            g = 2.0 * (d4[f, c, 9:41, :] + d4[f, c, 7:39, :]) - 8.0 * x
-            out = jnp.where(in_quad < 2, roll(x, -2), roll(x, 2))
-            out = out + jnp.where(in_quad == 1, roll(g, -1), jnp.where(in_quad == 2, roll(g, 1), 0.0))
-            out = -NU * out
-            if f == 0:
-                own = cs[0, c]
-                at_127 = 0.5 * (roll(own, -1) - roll(p_e, 1 - c))
-                at_0 = 0.5 * (roll(p_w, 2 - c) - roll(own, 1))
-                out = out + jnp.where(in_quad == 1, at_127, jnp.where(in_quad == 2, at_0, 0.0))
-            corr[f, c] = out
-
-    for name in ("uv_n", "uv_s", "p_n", "p_s"):
-        copies[name].wait_recv()
-
-    row = sublanes((R, C)) + lat * R
-    cor = ROT * (2.0 * (row.astype(F32) + 0.5) / NY - 1.0)
-    edge4 = (lane >= 126) | (lane < 2)
-
-    def stencil(f, k):
-        x = uv[f, k, 8:40, :]
-        one = uv[f, k, 9:41, :] + uv[f, k, 7:39, :]
-        two = uv[f, k, 10:42, :] + uv[f, k, 6:38, :]
-        far = -NU * x
-        near = (-2.0 * NU) * one - 8.0 * far
-        return x, far, near, -NU * two - 4.0 * near - 12.0 * far
-
-    sums = (zero,) * 4
-    for c in range(4):
-
-        def body(j, carry, c=c):
-            sgu, sgv, squ, sqv, acc = carry
-            k = c * CH + j
-            m = k < kmt
-            u0, ufar, unear, gu = stencil(0, k)
-            v0, vfar, vnear, gv = stencil(1, k)
-            hp = 0.5 * p[k, 8:40, :]
-            back = lax.rem(126 + C - 4 * j, C)
-            cu = roll(corr[0, c], back)
-            cv = roll(corr[1, c], back)
-            ue = roll(unear - hp, -1)
-            uw = roll(unear + hp, 1)
-            uee, uww = roll(ufar, -2), roll(ufar, 2)
-            ve, vw = roll(vnear, -1), roll(vnear, 1)
-            vee, vww = roll(vfar, -2), roll(vfar, 2)
-            gu = gu + cor * v0
-            gv = gv - cor * u0 - 0.5 * (p[k, 9:41, :] - p[k, 7:39, :])
-            gu = gu + jnp.where(edge4, cu, 0.0) + ((ue + uw) + (uee + uww))
-            gv = gv + jnp.where(edge4, cv, 0.0) + ((ve + vw) + (vee + vww))
-            gu = jnp.where(m, gu, 0.0)
-            gv = jnp.where(m, gv, 0.0)
-            qu = u0 + DT * gu
-            qv = v0 + DT * gv
-            q[0, k] = qu
-            q[1, k] = qv
-            h = s[0, k]
-            acc = jnp.where(quad == j, roll(qu, 4 * j + 2), acc)
-            return sgu + gu * h, sgv + gv * h, squ + qu * h, sqv + qv * h, acc
-
-        *sums, acc = lax.fori_loop(0, CH, body, (*sums, zero), unroll=UNROLL)
-        cs[0, c] = acc
+        cs[0, c] = q_edge[c]
     sgu, sgv, squ, sqv = sums
 
     bound = jnp.maximum(total, 1.0)
-    fu, fv = sgu / bound, sgv / bound
+    fu, fv = (1.0 / DT) * sgu / bound, (1.0 / DT) * sgv / bound
     a0u = -DT * fu - (squ - DT * fu * total) / bound
     a0v[...] = -DT * fv - (sqv - DT * fv * total) / bound
     b2[0, 40:72, :] = fu
@@ -377,9 +433,9 @@
     mine = [fu, fv, b2[2, 40:72, :], a0u]
     m2[0] = side(mine, True)
     m2[1] = side(mine, False)
+    send_sides("b2", m2, r2)
     send("b2_n", b2.at[:, 40:72, :], b2.at[:, 8:40, :], 0, 1)
     send("b2_s", b2.at[:, 40:72, :], b2.at[:, 72:104, :], 0, -1)
-    send_sides("b2", m2, r2)
     send("a_n", a0v.at[24:32, :], r_a0v.at[0], 0, 1)
     send("a_s", a0v.at[0:8, :], r_a0v.at[1], 0, -1)
     m_q[0] = compact(0, 1)
@@ -388,6 +444,10 @@
     send("q_w", m_q.at[1], r_q.at[1], -1, 0)
     send("q_n", q.at[1, :, 31, :], r_qrows.at[0], 0, 1)
     send("q_s", q.at[1, :, 0, :], r_qrows.at[1], 0, -1)
+    pack(scalars(2) + scalars(3))
+    send_scalars(range(4))
+    send("s_e", m_s.at[0], r_s.at[0], 1, 0)
+    send("s_w", m_s.at[1], r_s.at[1], -1, 0)
 
     for name in ("b2_n", "b2_s"):
         copies[name].wait_recv()
@@ -488,7 +548,7 @@
         cp.wait_send()
 
 
-N_COPIES = 2 + 6 + 2 + 4 + 2 + 6 + 4 + 2 + 6 + 2 + 4
+N_COPIES = 2 * (2 + 8 + 4) + 10 + 4 + 14
 
 
 def call_a(layers, kmt, baro):
@@ -505,9 +565,9 @@
         in_specs=[pl.BlockSpec(memory_space=pltpu.HBM)] * 3,
         out_specs=(vmem,) * 7,
         scratch_shapes=[
-            v(2, K, 48, C), v(K, 48, C), v(3, R, C), v(2, 4, 48, C), v(5, 4, R, C),
-            v(2, 4, R, C), v(2, 4, 48, C), v(2, R, C), v(2, R, C), v(2, 4, R, C), v(2, 4, R, C), v(2, R, C), v(2, R, C),
-            v(2, 4, 48, C), v(2, 4, R, C),
+            v(2, K, 48, C), v(K, 48, C), v(3, R, C), v(2, 4, 48, C), v(5, 4, R, C), v(4, R, C),
+            v(2, 4, R, C), v(2, 4, 48, C), v(2, 2, R, C), v(2, 2, R, C), v(2, 4, R, C), v(2, 4, R, C), v(2, R, C), v(2, R, C),
+            v(2, 4, 48, C), pltpu.VMEM((2, 4, R, 3 * C), BF16), pltpu.VMEM((5 * C, C), BF16),
             v(4, 112, C), v(2, R, C), v(2, 96, C), v(3, 112, C), v(2, R, C), v(2, 96, C),
             v(R, C), v(2, 8, C), v(2, 4, K, C), v(2, K, C),
             *surface, v(2, R, C), v(48, C),
@@ -516,9 +576,9 @@
             pltpu.SemaphoreType.DMA((N_COPIES,)),
         ],
         compiler_params=pltpu.CompilerParams(
-            collective_id=0, has_side_effects=True, vmem_limit_bytes=42 * 2**20),
+            collective_id=0, has_side_effects=True, vmem_limit_bytes=24 * 2**20),
         name="tendencies_and_surface",
-    )(layers, kmt, baro)
+    )(*(pltpu.with_memory_space_constraint(x, pltpu.HBM) for x in (layers, kmt, baro)))
 
 
 LB = 10
@@ -545,7 +605,7 @@
         r = [jnp.broadcast_to(halo, (8, C))] + [pltpu.roll(t, 1, axis=0) for t in tiles(x)]
         return jnp.concatenate([jnp.where(sub == 0, r[i], r[i + 1]) for i in range(4)], axis=0)
 
-    def body(k, carry):
+    def level(k):
         c = k // CH
         j = k - c * CH
         tile = k // (2 * CH)
@@ -563,10 +623,10 @@
             return roll(col[n, tile], back)
 
         def row_n(n):
-            return rows[4 + n, pl.ds(k, 1), :]
+            return rows[4 + n, k:k + 1, :]
 
         def row_s(n):
-            return rows[n, pl.ds(k, 1), :]
+            return rows[n, k:k + 1, :]
 
         hal = halo(0)
         e = jnp.where(lane == 127, hal, roll(fu, -1))
@@ -582,16 +642,18 @@
             w = jnp.where(lane == 0, hal, roll(x * kw, 1))
             r = from_north(x * kn, row_n(n)) + from_south(x * ks, row_s(n))
             out[2 + n, k] = jnp.where(m, (e + w) + (r + x * mid), 0.0)
-        return carry
+
+    def put(i):
+        at = slice(i * LB, (i + 1) * LB)
+        return pltpu.make_async_copy(out.at[:, at], out_hbm.at[:, at], out_sem.at[i])
 
     for i in range(K // LB):
-        at = slice(i * LB, (i + 1) * LB)
-        lax.fori_loop(i * LB, (i + 1) * LB, body, 0, unroll=UNROLL)
-        cp = pltpu.make_async_copy(out.at[:, at], out_hbm.at[:, at], out_sem.at[i])
-        cp.start()
-        copies.append(cp)
-    for cp in copies:
-        cp.wait()
+        for k in range(i * LB, (i + 1) * LB):
+            level(k)
+        put(i).start()
+    for i in range(K // LB):
+        put(i).wait()
+    copies[0].wait()
 
 
 def call_b(*operands):

time: 47.1 us -> 41.7 us (0.89)
  Pallas kernels: 44.7 us -> 40.9 us
  local copies, waits for them, and re-layouts: 1.51 us -> 0 us
    pallas_call x1, Pallas kernels: 36.8 us -> 34.6 us  [call_a(): pl.pallas_call(kernel_a, out_shape=(shape(2, K, R, C), shape(4, K, R, C),...]
    pallas_call x1, Pallas kernels: 7.87 us -> 6.34 us  [call_b(): pl.pallas_call(kernel_b, out_shape=(jax.ShapeDtypeStruct((6, K, R, C), F3...]
    unnamed x4 -> x0, local copies, waits for them, and re-layouts: 1.51 us -> none
where the time goes in v3:
time: 41.7 us; the launch traced here: 41.6 us
  Pallas kernels  40.9 us (98%)
  between operations  0.64 us (2%)
    pallas_call x1, Pallas kernels, call_a(): pl.pallas_call(kernel_a, out_shape=(shape(2, K, R, C), shape(4, K, R, C),...  34.6 us
    pallas_call x1, Pallas kernels, call_b(): pl.pallas_call(kernel_b, out_shape=(jax.ShapeDtypeStruct((6, K, R, C), F3...  6.34 us

profile of v3, /device:TPU:0, one launch (start us, length us, event | category | flops | bytes accessed | tf_op | source)
XLA Modules:
  0.0 41.6 jit_solution(12495325617929612760)
XLA Ops:
  0.6 34.6 %tendencies_and_surface.1 = (f32[2,100,32,128]{3,2,1,0:T(8,128)S(1)}, f32[4,100,32,128]{3,2,1,0:T(8,128)S(1)}, s32[32,128]{1,0:T(8,128)S(1)}, f32[2,32,128]{2,1,...) custom-call(f32[6,100,32,128]{3,2,1,0:T(8,128)} %layers.1, ...), custom_call_target="tpu_custom_call" | custom-call | tf_op jit(solution)/shard_map/tendencies_and_surface/pallas_call | solution.py:559
  35.2 6.3 %transport.1 = (f32[6,100,32,128]{3,2,1,0:T(8,128)}, f32[3,32,128]{2,1,0:T(8,128)}) custom-call(f32[2,100,32,128]{3,2,1,0:T(8,128)S(1)} %get-tuple-element.9.q, f32[4,100,32,128]{3,2,1,0:T(8,128)S(1)} %get-tuple-element.10.s, s32[32,128]{1,0:T(8,128)S(1)} %get-tuple-element.11.kmt_ref, f32[2,32,128]{2,1,0:T(8,128)S(1)} %get-tuple-element.12.a2d, ...), custom_call_target="tpu_custom_call" | custom-call | tf_op jit(solution)/shard_map/transport/pallas_call | solution.py:661

commit v4 on v3

--- a/solution.py
+++ b/solution.py
@@ -56,7 +56,7 @@
 def kernel_a(
     layers, kmt_hbm, baro_hbm,
     q, s, kmt_ref, a2d_out, baro_out, col_out, row_out,
-    uv, p, baro_ref, cuv, cs, q_edge,
+    uv, p, baro_ref, cuv, cs,
     m_uv, r_uv, m_p, r_p, m_s, r_s, m_q, r_q,
     d4, corr, shift,
     b1, m1, r1, b2, m2, r2, a0v, r_a0v, r_rows, r_qrows,
@@ -119,9 +119,6 @@
     loads["baro"].wait()
     kmt = kmt_ref[...]
     cmask = (kmt > 0).astype(F32)
-
-    for c in range(4):
-        q_edge[c] = jnp.zeros((R, C), F32)
 
     b1[1, 40:72, :] = baro_ref[1] * cmask
     b1[2, 40:72, :] = baro_ref[2] * cmask
@@ -373,7 +370,7 @@
     shift[...] = jnp.where(i < 2 * C, far, edge).astype(BF16)
     quad3 = lax.broadcasted_iota(jnp.int32, (1, 3 * C), 1) % C >> 2
 
-    def level(k, j, extra, sums, acc):
+    def level(k, extra, sums):
         sgu, sgv, squ, sqv = sums
         m = k < kmt
         kf = k.astype(F32)
@@ -394,8 +391,7 @@
         q[0, k] = qu
         q[1, k] = qv
         h = s[0, k]
-        acc = jnp.where(quad == j, roll(qu, 4 * j + 2), acc)
-        return (sgu + gu * h, sgv + gv * h, squ + qu * h, sqv + qv * h), acc
+        return sgu + gu * h, sgv + gv * h, squ + qu * h, sqv + qv * h
 
     sums = (zero,) * 4
     for i in range(2):
@@ -403,25 +399,25 @@
 
         def body(n, sums):
             c = n // 5
-            acc = zero
             j0 = 5 * (n - 5 * c)
-            left = []
+            left = [], []
             for l in range(5):
                 on = (quad3 == j0 + l).astype(F32).astype(BF16)
                 for f in range(2):
-                    left.append(jnp.concatenate([split(uv[f, 5 * n + l, 8:40, :], 2), corr[f, c] * on], axis=1))
-            moved = jnp.dot(jnp.concatenate(left, axis=0), shift[...], preferred_element_type=F32)
+                    deep = (5 - f) * C - 2 * C
+                    left[f].append(jnp.concatenate([split(uv[f, 5 * n + l, 8:40, :], 2), (corr[f, c] * on)[:, :deep]], axis=1))
+            moved = [
+                jnp.dot(jnp.concatenate(left[f], axis=0), shift[:(5 - f) * C, :], preferred_element_type=F32)
+                for f in range(2)
+            ]
             for l in range(5):
-                extra = [moved[R * (2 * l + f):R * (2 * l + f + 1)] for f in range(2)]
-                sums, acc = level(5 * n + l, j0 + l, extra, sums, acc)
-            q_edge[c] = q_edge[c] + acc
+                extra = [moved[f][R * l:R * (l + 1)] for f in range(2)]
+                sums = level(5 * n + l, extra, sums)
             return sums
 
         sums = lax.fori_loop(10 * i, 10 * i + 10, body, sums)
         if i == 0:
             prepare_surface()
-    for c in range(4):
-        cs[0, c] = q_edge[c]
     sgu, sgv, squ, sqv = sums
 
     bound = jnp.maximum(total, 1.0)
@@ -438,13 +434,14 @@
     send("b2_s", b2.at[:, 40:72, :], b2.at[:, 72:104, :], 0, -1)
     send("a_n", a0v.at[24:32, :], r_a0v.at[0], 0, 1)
     send("a_s", a0v.at[0:8, :], r_a0v.at[1], 0, -1)
+    send("q_n", q.at[1, :, 31, :], r_qrows.at[0], 0, 1)
+    send("q_s", q.at[1, :, 0, :], r_qrows.at[1], 0, -1)
+    pack([(lambda k: q[0, k], False, None, put_cs(0), c) for c in range(4)] + scalars(2))
     m_q[0] = compact(0, 1)
     m_q[1] = compact(0, 2)
     send("q_e", m_q.at[0], r_q.at[0], 1, 0)
     send("q_w", m_q.at[1], r_q.at[1], -1, 0)
-    send("q_n", q.at[1, :, 31, :], r_qrows.at[0], 0, 1)
-    send("q_s", q.at[1, :, 0, :], r_qrows.at[1], 0, -1)
-    pack(scalars(2) + scalars(3))
+    pack(scalars(3))
     send_scalars(range(4))
     send("s_e", m_s.at[0], r_s.at[0], 1, 0)
     send("s_w", m_s.at[1], r_s.at[1], -1, 0)
@@ -565,7 +562,7 @@
         in_specs=[pl.BlockSpec(memory_space=pltpu.HBM)] * 3,
         out_specs=(vmem,) * 7,
         scratch_shapes=[
-            v(2, K, 48, C), v(K, 48, C), v(3, R, C), v(2, 4, 48, C), v(5, 4, R, C), v(4, R, C),
+            v(2, K, 48, C), v(K, 48, C), v(3, R, C), v(2, 4, 48, C), v(5, 4, R, C),
             v(2, 4, R, C), v(2, 4, 48, C), v(2, 2, R, C), v(2, 2, R, C), v(2, 4, R, C), v(2, 4, R, C), v(2, R, C), v(2, R, C),
             v(2, 4, 48, C), pltpu.VMEM((2, 4, R, 3 * C), BF16), pltpu.VMEM((5 * C, C), BF16),
             v(4, 112, C), v(2, R, C), v(2, 96, C), v(3, 112, C), v(2, R, C), v(2, 96, C),

time: 41.7 us -> 39.6 us (0.950)
  Pallas kernels: 40.9 us -> 38.8 us
    pallas_call x1, Pallas kernels: 34.6 us -> 32.5 us  [call_a(): pl.pallas_call(kernel_a, out_shape=(shape(2, K, R, C), shape(4, K, R, C),...]
where the time goes in v4:
time: 39.6 us; the launch traced here: 39.4 us
  Pallas kernels  38.8 us (98%)
  between operations  0.64 us (2%)
    pallas_call x1, Pallas kernels, call_a(): pl.pallas_call(kernel_a, out_shape=(shape(2, K, R, C), shape(4, K, R, C),...  32.5 us
    pallas_call x1, Pallas kernels, call_b(): pl.pallas_call(kernel_b, out_shape=(jax.ShapeDtypeStruct((6, K, R, C), F3...  6.34 us

profile of v4, /device:TPU:0, one launch (start us, length us, event | category | flops | bytes accessed | tf_op | source)
XLA Modules:
  0.0 39.4 jit_solution(18386453281573202126)
XLA Ops:
  0.6 32.5 %tendencies_and_surface.1 = (f32[2,100,32,128]{3,2,1,0:T(8,128)S(1)}, f32[4,100,32,128]{3,2,1,0:T(8,128)S(1)}, s32[32,128]{1,0:T(8,128)S(1)}, f32[2,32,128]{2,1,...) custom-call(f32[6,100,32,128]{3,2,1,0:T(8,128)} %layers.1, ...), custom_call_target="tpu_custom_call" | custom-call | tf_op jit(solution)/shard_map/tendencies_and_surface/pallas_call | solution.py:556
  33.1 6.3 %transport.1 = (f32[6,100,32,128]{3,2,1,0:T(8,128)}, f32[3,32,128]{2,1,0:T(8,128)}) custom-call(f32[2,100,32,128]{3,2,1,0:T(8,128)S(1)} %get-tuple-element.9.q, f32[4,100,32,128]{3,2,1,0:T(8,128)S(1)} %get-tuple-element.10.s, s32[32,128]{1,0:T(8,128)S(1)} %get-tuple-element.11.kmt_ref, f32[2,32,128]{2,1,0:T(8,128)S(1)} %get-tuple-element.12.a2d, ...), custom_call_target="tpu_custom_call" | custom-call | tf_op jit(solution)/shard_map/transport/pallas_call | solution.py:658

commit v5 on v4

--- a/solution.py
+++ b/solution.py
@@ -415,7 +415,7 @@
                 sums = level(5 * n + l, extra, sums)
             return sums
 
-        sums = lax.fori_loop(10 * i, 10 * i + 10, body, sums)
+        sums = lax.fori_loop(10 * i, 10 * i + 10, body, sums, unroll=2)
         if i == 0:
             prepare_surface()
     sgu, sgv, squ, sqv = sums

time: 39.6 us -> 38.5 us (0.972)
  Pallas kernels: 38.8 us -> 37.7 us
    pallas_call x1, Pallas kernels: 32.5 us -> 31.4 us  [call_a(): pl.pallas_call(kernel_a, out_shape=(shape(2, K, R, C), shape(4, K, R, C),...]
where the time goes in v5:
time: 38.5 us; the launch traced here: 38.4 us
  Pallas kernels  37.7 us (98%)
  between operations  0.64 us (2%)
    pallas_call x1, Pallas kernels, call_a(): pl.pallas_call(kernel_a, out_shape=(shape(2, K, R, C), shape(4, K, R, C),...  31.4 us
    pallas_call x1, Pallas kernels, call_b(): pl.pallas_call(kernel_b, out_shape=(jax.ShapeDtypeStruct((6, K, R, C), F3...  6.34 us

profile of v5, /device:TPU:0, one launch (start us, length us, event | category | flops | bytes accessed | tf_op | source)
XLA Modules:
  0.0 38.4 jit_solution(13553107513749508764)
XLA Ops:
  0.6 31.4 %tendencies_and_surface.1 = (f32[2,100,32,128]{3,2,1,0:T(8,128)S(1)}, f32[4,100,32,128]{3,2,1,0:T(8,128)S(1)}, s32[32,128]{1,0:T(8,128)S(1)}, f32[2,32,128]{2,1,...) custom-call(f32[6,100,32,128]{3,2,1,0:T(8,128)} %layers.1, ...), custom_call_target="tpu_custom_call" | custom-call | tf_op jit(solution)/shard_map/tendencies_and_surface/pallas_call | solution.py:556
  32.0 6.3 %transport.1 = (f32[6,100,32,128]{3,2,1,0:T(8,128)}, f32[3,32,128]{2,1,0:T(8,128)}) custom-call(f32[2,100,32,128]{3,2,1,0:T(8,128)S(1)} %get-tuple-element.9.q, f32[4,100,32,128]{3,2,1,0:T(8,128)S(1)} %get-tuple-element.10.s, s32[32,128]{1,0:T(8,128)S(1)} %get-tuple-element.11.kmt_ref, f32[2,32,128]{2,1,0:T(8,128)S(1)} %get-tuple-element.12.a2d, ...), custom_call_target="tpu_custom_call" | custom-call | tf_op jit(solution)/shard_map/transport/pallas_call | solution.py:658
